TPU v7x, 256 devices: a whole 4x4x8 slice. The times are simulated.
256 devices in a mesh: kpt: 8 (over y_lo, x), band: 32 (over z, y_hi, core).
Axes of the slice: x: 4, y: 4 (y_hi: 2, y_lo: 2; y = y_hi * 2 + y_lo), z: 8, core: 2. Of those that a mesh axis runs over, the one named last changes fastest.
Arguments:
- targets: bfloat16 [8, 1, 2, 110592], P('kpt', None, None, 'band'), may hold values from -6 to 6
- sources: bfloat16 [8, 32, 2, 110592], P('kpt', 'band'), may hold values from -3 to 3
- kpt_coord: int32 [8, 3], replicated, may hold values from 0 to 3
Outputs:
- exchanged: float32 [8, 1, 2, 110592], P('kpt', None, None, 'band')
All inputs are finite; a program needn't handle non-finite values.
Results may differ from a plain program's by a relative error of at most 0.01.
Values may be sent and summed in bfloat16 or wider, within the bound.
A program may use at most 192 MiB of HBM per device.

v0:
```python
import math

import jax
import jax.numpy as jnp
from jax import lax
from jax.sharding import PartitionSpec as P

NG = 48


def passed_along(block, axis, distance):
    devices = range(lax.axis_size(axis))
    route = [((i - distance) % len(devices), i) for i in devices]
    return lax.ppermute(block, axis, route)


def tables(grid_len):
    grid_index = jnp.arange(grid_len, dtype=jnp.int32)
    products = grid_index[:, None] * grid_index[None, :] % grid_len
    phases = products.astype(jnp.float32) * (2.0 * math.pi / grid_len)
    cosine = jnp.cos(phases)
    sine_part = jnp.sin(phases)
    forward = jnp.stack([jnp.stack([cosine, sine_part]), jnp.stack([-sine_part, cosine])]).astype(
        jnp.bfloat16
    )
    backward = jnp.stack([jnp.stack([cosine, -sine_part]), jnp.stack([sine_part, cosine])]).astype(
        jnp.bfloat16
    )
    return (forward, backward)


def kernel(q_shift, grid_len):
    grid_index = jnp.arange(grid_len, dtype=jnp.int32)
    frequency = jnp.where(grid_index < grid_len // 2, grid_index, grid_index - grid_len).astype(
        jnp.float32
    )
    sq_x = (frequency + q_shift[0]) * (frequency + q_shift[0])
    sq_y = (frequency + q_shift[1]) * (frequency + q_shift[1])
    sq_z = (frequency + q_shift[2]) * (frequency + q_shift[2])
    wave_sq = sq_x[:, None, None] + sq_y[None, :, None] + sq_z[None, None, :]
    values_out = 4.0 * math.pi / (0.04 * wave_sq + 0.25) / float(grid_len * grid_len * grid_len)
    return values_out.reshape(-1)


def transform(values_in, matrix, grid_len):
    pair_count = values_in.shape[0]
    current = values_in.reshape(pair_count, 2, grid_len, grid_len * grid_len)
    result = None
    for section_num in range(3):
        result = jnp.einsum("pqmn,tqnc->tpcm", matrix, current, preferred_element_type=jnp.float32)
        if section_num < 2:
            current = result.astype(jnp.bfloat16).reshape(
                pair_count, 2, grid_len, grid_len * grid_len
            )
    return result.reshape(pair_count, 2, grid_len * grid_len * grid_len)


def contribution(source_block, targets_k, q_shift, forward, backward, grid_len):
    source_f = source_block.astype(jnp.float32)[:, None]
    targets_f = targets_k.astype(jnp.float32)[None]
    src_real = source_f[:, :, 0]
    src_imag = source_f[:, :, 1]
    tgt_real = targets_f[:, :, 0]
    tgt_imag = targets_f[:, :, 1]
    real_part = src_real * tgt_real + src_imag * tgt_imag
    imag_part = src_real * tgt_imag - src_imag * tgt_real
    density = jnp.stack([real_part, imag_part], axis=2).astype(jnp.bfloat16)
    band_count = density.shape[0]
    target_count = density.shape[1]
    cells = density.shape[3]
    density = density.reshape(band_count * target_count, 2, cells)
    spectrum = transform(density, forward, grid_len)
    screened = (spectrum * kernel(q_shift, grid_len)).astype(jnp.bfloat16)
    potential = transform(screened, backward, grid_len).reshape(band_count, target_count, 2, cells)
    pot_real = potential[:, :, 0]
    pot_imag = potential[:, :, 1]
    out_real = jnp.sum(src_real * pot_real - src_imag * pot_imag, axis=0)
    out_imag = jnp.sum(src_real * pot_imag + src_imag * pot_real, axis=0)
    return jnp.stack([out_real, out_imag], axis=1)


def per_device(targets, sources, kpt_coord):
    forward, backward = tables(NG)
    whole_targets = lax.all_gather(targets[0], "band", axis=2, tiled=True)
    my_group = lax.axis_index("kpt")
    kgroups = lax.axis_size("kpt")

    def accumulate(summed, source_block, anchor):
        q_shift = (kpt_coord[my_group] - kpt_coord[anchor]).astype(jnp.float32) * 0.25
        return summed + contribution(source_block[0], whole_targets, q_shift, forward, backward, NG)

    summed = jnp.zeros(whole_targets.shape, jnp.float32)
    summed = accumulate(summed, sources, my_group)
    moving = sources
    for step_num in range(1, kgroups):
        moving = passed_along(moving, "kpt", 1)
        summed = accumulate(summed, moving, (my_group - step_num) % kgroups)
    shares = lax.psum_scatter(
        (summed * (-1.0 / kgroups)).astype(jnp.bfloat16), "band", scatter_dimension=2, tiled=True
    ).astype(jnp.float32)
    return shares[None]


def solution(mesh):
    in_specs = (P("kpt", None, None, "band"), P("kpt", "band", None, None), P())
    out_specs = P("kpt", None, None, "band")
    return jax.shard_map(
        per_device, mesh=mesh, in_specs=in_specs, out_specs=out_specs, check_vma=False
    )
```

profile of v0, /device:TPU:1, one launch (start us, length us, event | category | flops | bytes accessed | tf_op | source)
XLA Modules:
  0.0 832.3 jit_solution(5730774102440857966)
XLA Ops:
  6.5 2.0 collective-permute-start
  32.2 47.0 %all-gather = bf16[1,1,2,110592]{3,2,1,0:T(2,128)(2,1)S(1)} all-gather(bf16[1,1,2,3456]{3,2,1,0:T(2,128)(2,1)S(1)} %copy-done.38), channel_id=2, replica_groups=mesh['kpt'=8,'band'=32] {'band'}, dimensions={3}, use_global_device_ids=true | all-gather | bytes 456192 | tf_op jit(solution)/shard_map/all_gather | solution.py:84
  99.4 11.8 %collective-permute-done.1 = bf16[1,1,2,110592]{3,2,1,0:T(2,128)(2,1)S(1)} collective-permute-done((bf16[1,1,2,110592]{3,2,1,0:T(2,128)(2,1)}, bf16[1,1,2,110592]{3,2,1,0:T(2,128)(2,1)S(1)}, u32[]{:S(2)}, u32[]{:S(2)}) %collective-permute-start.1) | collective-permute-done | bytes 442400 | tf_op jit(solution)/shard_map/ppermute | solution.py:14
  112.1 11.9 %collective-permute-done.2 = bf16[1,1,2,110592]{3,2,1,0:T(2,128)(2,1)S(1)} collective-permute-done((bf16[1,1,2,110592]{3,2,1,0:T(2,128)(2,1)S(1)}, bf16[1,1,2,110592]{3,2,1,0:T(2,128)(2,1)S(1)}, u32[]{:S(2)}, u32[]{:S(2)}) %collective-permute-start.2) | collective-permute-done | bytes 442400 | tf_op jit(solution)/shard_map/ppermute | solution.py:14
  124.9 11.0 %collective-permute-done.3 = bf16[1,1,2,110592]{3,2,1,0:T(2,128)(2,1)S(1)} collective-permute-done((bf16[1,1,2,110592]{3,2,1,0:T(2,128)(2,1)S(1)}, bf16[1,1,2,110592]{3,2,1,0:T(2,128)(2,1)S(1)}, u32[]{:S(2)}, u32[]{:S(2)}) %collective-permute-start.3) | collective-permute-done | bytes 442400 | tf_op jit(solution)/shard_map/ppermute | solution.py:14
  139.3 7.8 collective-permute-done.4
  148.2 25.8 %convert_reduce_fusion.15 = (bf16[110592]{0:T(1024)(128)(2,1)}, bf16[110592]{0:T(1024)(128)(2,1)}, bf16[110592]{0:T(1024)(128)(2,1)}, bf16[110592]{0:T(1024)(128...) fusion(f32[1,1,2,110592]{3,2,1,0:T(2,128)S(1)} %convert_element, ...), kind=kLoop, calls=%fused_computation.210 | loop fusion | flops 5308416 | bytes 8847360 | tf_op jit(solution)/shard_map/convert.49
  236.5 2.9 reshape_reshape.32
  239.4 4.3 subtract_bitcast_fusion.7
  256.8 2.9 reshape_reshape.33
  259.7 4.3 subtract_bitcast_fusion.6
  275.1 2.2 copy.87
  277.3 2.9 reshape_reshape.37
  280.2 4.2 subtract_bitcast_fusion.2
  297.5 2.9 reshape_reshape.36
  300.4 4.3 subtract_bitcast_fusion.3
  315.7 2.0 copy.75
  317.7 2.9 reshape_reshape.35
  320.6 4.4 subtract_bitcast_fusion.4
  337.8 2.9 reshape_reshape.34
  341.2 4.3 subtract_bitcast_fusion.5
  346.8 4.6 collective-permute-done.6
  351.8 8.0 convert_reduce_fusion.3
  389.2 2.9 reshape_reshape.38
  392.1 4.4 subtract_bitcast_fusion.1
  409.5 2.9 reshape_reshape.39
  412.5 2.7 subtract_bitcast_fusion
  415.3 7.2 fusion.70
  422.5 84.2 %copy.148 = bf16[1,2,110592]{1,0,2:T(2,128)(2,1)} copy(bf16[1,2,110592]{2,1,0:T(2,128)(2,1)S(1)} %fusion.70) | data formatting | bytes 884736
  506.7 28.5 %copy.152 = bf16[110592,1,2]{2,0,1:T(8,128)(2,1)} copy(bf16[110592,1,2]{2,1,0:T(2,128)(2,1)} %bitcast.694) | data formatting | bytes 884736
  535.3 284.9 %reduce-scatter.4.cloned.1.call-done = bf16[3456,2]{1,0:T(8,128)(2,1)} async-done(((bf16[110592,2]{1,0:T(8,128)(2,1)}), bf16[3456,2]{1,0:T(8,128)(2,1)}) %reduce-scatter.4.cloned.1.call-update) | async-done | bytes 13840
  820.2 2.6 reshape_bitcast_fusion
  (348 shorter events, 219.3 us)
Async XLA Ops:
  6.5 4.3 copy-start.35
  6.5 25.7 %copy-start.38 = (bf16[1,1,2,3456]{3,2,1,0:T(2,128)(2,1)S(1)}, bf16[1,1,2,3456]{3,2,1,0:T(2,128)(2,1)}, u32[]{:S(2)}) copy-start(bf16[1,1,2,3456]{3,2,1,0:T(2,128)(2,1)} %param.3) | copy-start | bytes 41476
  6.5 813.7 %reduce-scatter.4.cloned.1.call-start = ((), (), s32[]{:S(2)}) async-start(), calls=%async_computation.1 | async-start | bytes 29196288
  6.5 90.7 %collective-permute-start = (bf16[1,1,2,110592]{3,2,1,0:T(2,128)(2,1)}, bf16[1,1,2,110592]{3,2,1,0:T(2,128)(2,1)}, u32[]{:S(2)}, u32[]{:S(2)}) collective-permute-start(bf16[1,1,2,110592]{3,2,1,0:T(2,128)(2,1)} %param.4), channel_id=1, source_target_pairs={{224,0},{0,32},{32,64},{64,96},{96,128},{128,160},{160,192},{192,2... | collective-permute-start | bytes 1327112 | tf_op jit(solution)/shard_map/ppermute | solution.py:14
  10.8 137.4 %copy-start = (f32[1,1,2,110592]{3,2,1,0:T(2,128)}, f32[1,1,2,110592]{3,2,1,0:T(2,128)S(1)}, u32[]{:S(2)}) copy-start(f32[1,1,2,110592]{3,2,1,0:T(2,128)S(1)} %convert_element_type.643) | copy-start | bytes 2654212
  93.6 2.8 copy-start.36
  93.6 2.8 copy-start.37
  95.5 3.0 copy-start.11
  96.4 14.9 %copy-start.10 = (f32[48,2304]{1,0:T(8,128)S(1)}, f32[48,2304]{1,0:T(8,128)}, u32[]{:S(2)}) copy-start(f32[48,2304]{1,0:T(8,128)} %add.1195) | copy-start | bytes 1327108
  96.4 27.7 %copy-start.8 = (f32[48,2304]{1,0:T(8,128)S(1)}, f32[48,2304]{1,0:T(8,128)}, u32[]{:S(2)}) copy-start(f32[48,2304]{1,0:T(8,128)} %add.1216) | copy-start | bytes 1327108
  97.3 38.8 %copy-start.7 = (f32[48,2304]{1,0:T(8,128)S(1)}, f32[48,2304]{1,0:T(8,128)}, u32[]{:S(2)}) copy-start(f32[48,2304]{1,0:T(8,128)} %add.1237) | copy-start | bytes 1327108
  97.3 13.9 %collective-permute-start.1 = (bf16[1,1,2,110592]{3,2,1,0:T(2,128)(2,1)}, bf16[1,1,2,110592]{3,2,1,0:T(2,128)(2,1)S(1)}, u32[]{:S(2)}, u32[]{:S(2)}) collective-permute-start(bf16[1,1,2,110592]{3,2,1,0:T(2,128)(2,1)} %collective-permute-done), channel_id=1, source_target_pairs={{224,0},{0,32},{32,64},{64,96},{96,128},{128,160},{160,192},{192,2... | collective-permute-start | bytes 1327112 | tf_op jit(solution)/shard_map/ppermute | solution.py:14
  111.2 12.8 %collective-permute-start.2 = (bf16[1,1,2,110592]{3,2,1,0:T(2,128)(2,1)S(1)}, bf16[1,1,2,110592]{3,2,1,0:T(2,128)(2,1)S(1)}, u32[]{:S(2)}, u32[]{:S(2)}) collective-permute-start(bf16[1,1,2,110592]{3,2,1,0:T(2,128)(2,1)S(1)} %collective-permute-done.1), channel_id=1, source_target_pairs={{224,0},{0,32},{32,64},{64,96},{96,128},{128,160},{160,192},{192,2... | collective-permute-start | bytes 1327112 | tf_op jit(solution)/shard_map/ppermute | solution.py:14
  124.0 11.9 %collective-permute-start.3 = (bf16[1,1,2,110592]{3,2,1,0:T(2,128)(2,1)S(1)}, bf16[1,1,2,110592]{3,2,1,0:T(2,128)(2,1)S(1)}, u32[]{:S(2)}, u32[]{:S(2)}) collective-permute-start(bf16[1,1,2,110592]{3,2,1,0:T(2,128)(2,1)S(1)} %collective-permute-done.2), channel_id=1, source_target_pairs={{224,0},{0,32},{32,64},{64,96},{96,128},{128,160},{160,192},{192,2... | collective-permute-start | bytes 1327112 | tf_op jit(solution)/shard_map/ppermute | solution.py:14
  135.9 11.1 %collective-permute-start.4 = (bf16[1,1,2,110592]{3,2,1,0:T(2,128)(2,1)S(1)}, bf16[1,1,2,110592]{3,2,1,0:T(2,128)(2,1)S(1)}, u32[]{:S(2)}, u32[]{:S(2)}) collective-permute-start(bf16[1,1,2,110592]{3,2,1,0:T(2,128)(2,1)S(1)} %collective-permute-done.3), channel_id=1, source_target_pairs={{224,0},{0,32},{32,64},{64,96},{96,128},{128,160},{160,192},{192,2... | collective-permute-start | bytes 1327112 | tf_op jit(solution)/shard_map/ppermute | solution.py:14
  138.3 9.9 %copy-start.5 = (f32[1,1,2,110592]{3,2,1,0:T(2,128)}, f32[1,1,2,110592]{3,2,1,0:T(2,128)S(1)}, u32[]{:S(2)}) copy-start(f32[1,1,2,110592]{3,2,1,0:T(2,128)S(1)} %convert_element_type.659) | copy-start | bytes 2654212
  138.6 9.5 %copy-start.1 = (f32[1,1,2,110592]{3,2,1,0:T(2,128)}, f32[1,1,2,110592]{3,2,1,0:T(2,128)S(1)}, u32[]{:S(2)}) copy-start(f32[1,1,2,110592]{3,2,1,0:T(2,128)S(1)} %convert_element_type.674) | copy-start | bytes 2654212
  138.9 9.2 %copy-start.2 = (f32[1,1,2,110592]{3,2,1,0:T(2,128)}, f32[1,1,2,110592]{3,2,1,0:T(2,128)S(1)}, u32[]{:S(2)}) copy-start(f32[1,1,2,110592]{3,2,1,0:T(2,128)S(1)} %convert_element_type.689) | copy-start | bytes 2654212
  139.3 34.7 %copy-start.3 = (f32[1,1,2,110592]{3,2,1,0:T(2,128)}, f32[1,1,2,110592]{3,2,1,0:T(2,128)S(1)}, u32[]{:S(2)}) copy-start(f32[1,1,2,110592]{3,2,1,0:T(2,128)S(1)} %convert_element_type.704) | copy-start | bytes 2654212
  148.2 25.8 %copy-start.4 = (f32[1,1,2,110592]{3,2,1,0:T(2,128)}, f32[1,1,2,110592]{3,2,1,0:T(2,128)S(1)}, u32[]{:S(2)}) copy-start(f32[1,1,2,110592]{3,2,1,0:T(2,128)S(1)} %convert_element_type.719) | copy-start | bytes 2654212
  174.0 5.8 copy-start.22
  174.0 6.7 copy-start.21
  174.0 7.7 copy-start.20
  328.7 12.0 %collective-permute-start.5 = (bf16[1,1,2,110592]{3,2,1,0:T(2,128)(2,1)}, bf16[1,1,2,110592]{3,2,1,0:T(2,128)(2,1)}, u32[]{:S(2)}, u32[]{:S(2)}) collective-permute-start(bf16[1,1,2,110592]{3,2,1,0:T(2,128)(2,1)} %copy-done.23), channel_id=1, source_target_pairs={{224,0},{0,32},{32,64},{64,96},{96,128},{128,160},{160,192},{192,2... | collective-permute-start | bytes 1327112 | tf_op jit(solution)/shard_map/ppermute | solution.py:14
  340.8 10.7 %collective-permute-start.6 = (bf16[1,1,2,110592]{3,2,1,0:T(2,128)(2,1)}, bf16[1,1,2,110592]{3,2,1,0:T(2,128)(2,1)S(1)}, u32[]{:S(2)}, u32[]{:S(2)}) collective-permute-start(bf16[1,1,2,110592]{3,2,1,0:T(2,128)(2,1)} %collective-permute-done.5), channel_id=1, source_target_pairs={{224,0},{0,32},{32,64},{64,96},{96,128},{128,160},{160,192},{192,2... | collective-permute-start | bytes 1327112 | tf_op jit(solution)/shard_map/ppermute | solution.py:14
  346.8 13.0 %copy-start.6 = (f32[1,1,2,110592]{3,2,1,0:T(2,128)}, f32[1,1,2,110592]{3,2,1,0:T(2,128)S(1)}, u32[]{:S(2)}) copy-start(f32[1,1,2,110592]{3,2,1,0:T(2,128)S(1)} %convert_element_type.734) | copy-start | bytes 2654212
  412.5 2.8 copy-start.14
  412.5 2.8 copy-start.15
  412.5 2.8 copy-start.16
  412.5 2.8 copy-start.17
  412.5 2.8 copy-start.18
  412.5 2.8 copy-start.19
  (26 other events, 50.9 us)
Sparse Core Ops, SparseCore 0:
  535.4 284.7 reduce-scatter.3
where the time goes:
time: 842 us; the launch traced here: 832 us
  waiting for transfers between devices  332 us (39%)
  local copies, waits for them, and re-layouts  286 us (34%)
  other arithmetic  108 us (13%)
  blocking collectives  47 us (6%)
  matrix products  40.6 us (5%)
  between operations  14.9 us (2%)
    unnamed x2, waiting for transfers between devices  285 us
    unnamed x104, local copies, waits for them, and re-layouts  118 us
    ppermute x7, waiting for transfers between devices, passed_along(): return lax.ppermute(block, axis, route)  47.2 us
    all_gather x1, blocking collectives, per_device(): whole_targets = lax.all_gather(targets[0], 'band', axis=2, tiled=True)  47 us
    another operation x32, local copies, waits for them, and re-layouts  42.9 us
    dot_general x48, matrix products, transform(): jnp.einsum('pqmn,tqnc->tpcm', matrix, current, preferred_element_type=jnp...  40.6 us
    another operation x4, other arithmetic  34.6 us
    another operation x8, other arithmetic, contribution(): return jnp.stack([out_real, out_imag], axis=1)  32.9 us
  transfers between devices with their start and end apart: 8, of which 6 were waited for; matrix products, arithmetic and copies ran while one was open for 8% of the time, Pallas kernels for 0%

commit v1 on v0

v1 whole, which is shorter than its diff:
```python
import functools
import math

import jax
import jax.numpy as jnp
import ml_dtypes
import numpy as np
from jax import lax
from jax.experimental import pallas as pl
from jax.experimental.pallas import tpu as pltpu
from jax.sharding import PartitionSpec as P

NG = 48
ROWS = 2 * NG
PITCH = 104
GROUP1 = 12
GROUP2 = 12
GROUP3 = 12
BF16 = jnp.bfloat16
F32 = jnp.float32
MESH = pl.DeviceIdType.MESH


def host_tables():
    index = np.arange(NG)
    phases = ((index[:, None] * index[None, :]) % NG).astype(np.float32) * np.float32(2.0 * math.pi / NG)
    half = ml_dtypes.bfloat16
    cosine = np.cos(phases).astype(half).astype(np.float32)
    sine = np.sin(phases).astype(half).astype(np.float32)
    forward = np.block([[cosine, sine], [-sine, cosine]])
    backward = np.block([[cosine, -sine], [sine, cosine]])

    def lane_table(table):
        wide = np.zeros((2, 2, 64, 2, 2, 64), np.float32)
        for p in range(2):
            for q in range(2):
                for t in range(2):
                    wide[p, t, :NG, q, t, :NG] = table[q * NG:(q + 1) * NG, p * NG:(p + 1) * NG].T
        return wide.reshape(256, 256)

    spread = np.zeros((2, 4, 256, 2, 2, 64), np.float32)
    gather = np.zeros((3, 4, 2, 64, 2, 128), np.float32)
    first_lane = [0, 0, 128, 128]
    for k in range(8):
        for z in range(NG):
            for t in range(2):
                spread[t, k // 2, 48 * k + z - first_lane[k // 2], k % 2, t, z] = 1
                for chunk in range(3):
                    lane = 48 * k + z - 128 * chunk
                    if 0 <= lane < 128:
                        gather[chunk, k - 2 * chunk, t, z, t, lane] = 1
    return [
        a.astype(half)
        for a in (
            forward,
            backward,
            lane_table(forward),
            lane_table(backward),
            spread.reshape(2, 4, 256, 256),
            gather.reshape(3, 512, 256),
        )
    ]


def dot(a, b):
    return jnp.dot(a, b, preferred_element_type=F32)


def exchange(
    kpt_ref, slice_ref, source_ref, fwd_ref, bwd_ref, zfwd_ref, zbwd_ref, spread_ref, gather_ref, out_ref,
    slots, rows_f32, dense, targ, sources, src, work1, work2, coul, total,
    sums_b, recv_c, sums_c, recv_y, sums_y, recv_z,
    gz_send, gz_recv, gy_send, gy_recv, gc_send, gc_recv, s_send, s_recv,
    rc_send, rc_recv, ry_send, ry_recv, rz_send, rz_recv,
):
    kpt = lax.axis_index("kpt")
    band = lax.axis_index("band")
    x = kpt % 4
    y = (kpt // 4) * 2 + (band // 2) % 2
    z = band // 4
    c = band % 2

    def device(x_, y_, z_, c_):
        return ((y_ // 2) * 4 + x_, z_ * 4 + (y_ % 2) * 2 + c_)

    def push(source, target, send, recv, where):
        copy = pltpu.make_async_remote_copy(
            src_ref=source, dst_ref=target, send_sem=send, recv_sem=recv, device_id=where, device_id_type=MESH
        )
        copy.start()
        return copy

    x_up = device((x + 1) % 4, y, z, c)
    x_down = device((x + 3) % 4, y, z, c)
    other = device(x, y, z, 1 - c)
    z_at = [device(x, y, (z + d) % 8, c) for d in range(8)]
    y_at = [device(x, (y + d) % 4, z, c) for d in range(4)]

    barrier = pltpu.get_barrier_semaphore()
    for peer in [x_up, x_down, other] + z_at[1:] + y_at[1:]:
        pl.semaphore_signal(barrier, inc=1, device_id=peer, device_id_type=MESH)
    pl.semaphore_wait(barrier, 13)

    to_up = push(source_ref, sources.at[1], s_send.at[0], s_recv.at[0], x_up)
    to_down = push(source_ref, sources.at[2], s_send.at[1], s_recv.at[1], x_down)

    slots[y, c, z] = slice_ref[...]
    along_z = [
        push(slots.at[y, c, z], slots.at[y, c, z], gz_send.at[d - 1], gz_recv.at[d - 1], z_at[d])
        for d in range(1, 8)
    ]
    sources[0] = source_ref[...]
    total[...] = jnp.zeros_like(total)
    for copy in along_z:
        copy.wait_recv()
    along_y = [
        push(slots.at[y, c], slots.at[y, c], gy_send.at[d - 1], gy_recv.at[d - 1], y_at[d])
        for d in range(1, 4)
    ]
    across = [push(slots.at[y, c], slots.at[y, c], gc_send.at[0], gc_recv.at[0], other)]
    for d in range(1, 4):
        along_y[d - 1].wait_recv()
        from_y = (y + 4 - d) % 4
        across.append(
            push(slots.at[from_y, c], slots.at[from_y, c], gc_send.at[d], gc_recv.at[d], other)
        )
    for copy in across:
        copy.wait_recv()

    def unpack(w, carry):
        for t in range(2):
            piece = slots[t * 2 + (w // 2) % 2, w % 2, w // 4].astype(F32)
            for p in range(2):
                rows_f32[t, pl.ds(p * 864 + 27 * w, 27), :] = piece[p * 32:p * 32 + 27]
        return carry

    lax.fori_loop(0, 32, unpack, 0)
    for t in range(2):
        for p in range(2):
            for col in range(18):
                dense[t, p * NG:(p + 1) * NG, col * 128:(col + 1) * 128] = rows_f32[
                    t, pl.ds(p * 864 + col, NG, stride=18), :
                ].astype(BF16)

    lane_from = [0, 0, 128, 256]
    table_rows = [slice(0, 128), slice(0, 256), slice(0, 256), slice(128, 256)]

    def spread_out(read, tables, store):
        for g in range(6):
            for k in range(4):
                width = 128 if k in (0, 3) else 256
                lanes = slice(384 * g + lane_from[k], 384 * g + lane_from[k] + width)
                wide = sum(
                    dot(read(i, lanes), tables(i, k, table_rows[k])) for i in range(2 if store is targ else 1)
                ).astype(BF16)
                store[8 * g + 2 * k] = wide[:, :128]
                store[8 * g + 2 * k + 1] = wide[:, 128:]

    spread_out(lambda t, lanes: dense[t, :, lanes], lambda t, k, r: spread_ref[t, k, r, :], targ)

    lane = lax.broadcasted_iota(jnp.int32, (NG, 128), 1)
    row = lax.broadcasted_iota(jnp.int32, (NG, 128), 0)
    first = lane < 64

    def frequency(i):
        return jnp.where(i < NG // 2, i, i - NG).astype(F32)

    scale = 4.0 * math.pi / float(NG**3)
    forward = fwd_ref[...]
    backward = bwd_ref[...]
    zforward = zfwd_ref[...]
    zbackward = zbwd_ref[...]

    def step(num, carry):
        @pl.when(num == 1)
        def _():
            to_up.wait_recv()
            to_down.wait_recv()
            push(sources.at[1, pl.ds(0, NG)], sources.at[3, pl.ds(0, NG)], s_send.at[2], s_recv.at[2], x_up)
            push(sources.at[2, pl.ds(NG, NG)], sources.at[3, pl.ds(NG, NG)], s_send.at[3], s_recv.at[3], x_down)

        @pl.when(num == 3)
        def _():
            for half in range(2):
                part = sources.at[3, pl.ds(half * NG, NG)]
                pltpu.make_async_remote_copy(
                    src_ref=part, dst_ref=part, send_sem=s_send.at[2 + half], recv_sem=s_recv.at[2 + half],
                    device_id=x_up if half == 0 else x_down, device_id_type=MESH,
                ).wait()

        spread_out(
            lambda i, lanes: sources[num, :, lanes],
            lambda i, k, r: spread_ref[0, k, r, :] + spread_ref[1, k, r, :],
            src,
        )
        from_k = (kpt // 4) * 4 + (x + jnp.where(num == 0, 0, jnp.where(num == 1, 3, jnp.where(num == 2, 1, 2)))) % 4

        def offset(d):
            own = kpt_ref[from_k, d]
            return jnp.where(first, kpt_ref[x, d] - own, kpt_ref[x + 4, d] - own).astype(F32) * 0.25

        fx = frequency(row) + offset(0)
        fy = frequency(row) + offset(1)
        fz = frequency(lane % 64) + offset(2)
        coul[...] = 0.04 * (fx * fx)
        fyz = 0.04 * (fy * fy + fz * fz) + 0.25

        def into_spectrum(i, carry):
            mixed = []
            for j in range(GROUP1):
                pair = []
                for cell in (2 * (i * GROUP1 + j), 2 * (i * GROUP1 + j) + 1):
                    s = src[cell].astype(F32)
                    t = targ[cell].astype(F32)
                    sr, si, tr, ti = s[:NG], s[NG:], t[:NG], t[NG:]
                    pair.append(
                        jnp.concatenate([(sr * tr + si * ti).astype(BF16), (sr * ti - si * tr).astype(BF16)], axis=0)
                    )
                after_x = dot(forward, jnp.concatenate(pair, axis=1)).astype(BF16)
                for h in (0, 128):
                    mixed.append(jnp.concatenate([after_x[:NG, h:h + 128], after_x[NG:, h:h + 128]], axis=1))
            after_z = dot(jnp.concatenate(mixed, axis=0), zforward)
            for j in range(2 * GROUP1):
                for p in range(2):
                    start = (2 * i * GROUP1 + j) * PITCH + p * NG
                    work1[pl.ds(start, NG), :] = after_z[j * NG:(j + 1) * NG, p * 128:p * 128 + 128]
            return carry

        def through_spectrum(i, carry):
            for j in range(GROUP2):
                cells = (2 * (i * GROUP2 + j), 2 * (i * GROUP2 + j) + 1)
                pair = [
                    jnp.concatenate(
                        [work1[pl.ds(cell + p * NG, NG, stride=PITCH), :].astype(BF16) for p in range(2)], axis=0
                    )
                    for cell in cells
                ]
                spectrum = dot(forward, jnp.concatenate(pair, axis=1))
                pair = []
                for h, cell in enumerate(cells):
                    factor = scale / (fyz + coul[pl.ds(cell, 1), :])
                    part = spectrum[:, h * 128:h * 128 + 128]
                    pair.append(
                        jnp.concatenate([(part[:NG] * factor).astype(BF16), (part[NG:] * factor).astype(BF16)], axis=0)
                    )
                after_y = dot(backward, jnp.concatenate(pair, axis=1))
                for h, cell in enumerate(cells):
                    work2[pl.ds(cell * PITCH, ROWS), :] = after_y[:, h * 128:h * 128 + 128]
            return carry

        def out_of_spectrum(i, carry):
            mixed = [
                jnp.concatenate(
                    [
                        work2[pl.ds(2 * i * GROUP3 + j + p * NG, NG, stride=PITCH), :].astype(BF16)
                        for p in range(2)
                    ],
                    axis=1,
                )
                for j in range(2 * GROUP3)
            ]
            after_z = dot(jnp.concatenate(mixed, axis=0), zbackward).astype(BF16)
            for j in range(GROUP3):
                pair = [
                    jnp.concatenate([after_z[n * NG:(n + 1) * NG, :128], after_z[n * NG:(n + 1) * NG, 128:]], axis=0)
                    for n in (2 * j, 2 * j + 1)
                ]
                potential = dot(backward, jnp.concatenate(pair, axis=1))
                for h in range(2):
                    cell = 2 * (i * GROUP3 + j) + h
                    s = src[cell].astype(F32)
                    sr, si = s[:NG], s[NG:]
                    pr = potential[:NG, h * 128:h * 128 + 128]
                    pi = potential[NG:, h * 128:h * 128 + 128]
                    total[cell, :NG, :] += sr * pr - si * pi
                    total[cell, NG:, :] += sr * pi + si * pr
            return carry

        lax.fori_loop(0, 24 // GROUP1, into_spectrum, 0)
        lax.fori_loop(0, 24 // GROUP2, through_spectrum, 0)
        lax.fori_loop(0, 24 // GROUP3, out_of_spectrum, 0)
        return carry

    lax.fori_loop(0, 4, step, 0)

    for g in range(6):
        for chunk in range(3):
            cells = [8 * g + 2 * chunk + k for k in range(4)]
            narrow = dot(jnp.concatenate([total[n].astype(BF16) for n in cells], axis=1), gather_ref[chunk])
            for t in range(2):
                for p in range(2):
                    rows_f32[t, pl.ds(p * 864 + 3 * g + chunk, NG, stride=18), :] = narrow[
                        p * NG:(p + 1) * NG, t * 128:t * 128 + 128
                    ]

    def pack(w, carry):
        for t in range(2):
            for p in range(2):
                sums_b[t * 2 + (w // 2) % 2, w % 2, w // 4, p * 32:p * 32 + 32, :] = rows_f32[
                    t, pl.ds(p * 864 + 27 * w, 32), :
                ].astype(BF16)
        return carry

    lax.fori_loop(0, 32, pack, 0)

    across2 = [
        push(sums_b.at[(y + d) % 4, 1 - c], recv_c.at[(y + d) % 4], rc_send.at[d], rc_recv.at[d], other)
        for d in range(4)
    ]
    along_y2 = []
    for d in (1, 2, 3, 0):
        across2[d].wait_recv()
        to_y = (y + d) % 4
        sums_c[to_y] = (sums_b[to_y, c].astype(F32) + recv_c[to_y].astype(F32)).astype(BF16)
        if d:
            along_y2.append(push(sums_c.at[to_y], recv_y.at[d - 1], ry_send.at[d - 1], ry_recv.at[d - 1], y_at[d]))
    for copy in along_y2:
        copy.wait_recv()
    sums_y[...] = sum([recv_y[d].astype(F32) for d in range(3)], sums_c[y].astype(F32)).astype(BF16)
    along_z2 = [
        push(sums_y.at[(z + d) % 8], recv_z.at[d - 1], rz_send.at[d - 1], rz_recv.at[d - 1], z_at[d])
        for d in range(1, 8)
    ]
    for copy in along_z2:
        copy.wait_recv()
    result = sum([recv_z[d].astype(F32) for d in range(7)], sums_y[z].astype(F32)) * (-1.0 / 8.0)
    out_ref[...] = result

    for copy in [to_up, to_down] + along_z + along_y + across + across2 + along_y2 + along_z2:
        copy.wait_send()


def per_device(targets, sources, kpt_coord):
    piece = jnp.pad(targets.reshape(2, 27, 128), ((0, 0), (0, 5), (0, 0))).reshape(64, 128)
    source = sources.reshape(ROWS, NG * NG)
    tables = [jnp.asarray(a) for a in host_tables()]
    vmem = pl.BlockSpec(memory_space=pltpu.VMEM)
    sems = pltpu.SemaphoreType.DMA
    out = pl.pallas_call(
        exchange,
        in_specs=[pl.BlockSpec(memory_space=pltpu.SMEM)] + [vmem] * 8,
        out_specs=vmem,
        out_shape=jax.ShapeDtypeStruct((64, 128), F32),
        scratch_shapes=[
            pltpu.VMEM((4, 2, 8, 64, 128), BF16),
            pltpu.VMEM((2, 1736, 128), F32),
            pltpu.VMEM((2, ROWS, NG * NG), BF16),
            pltpu.VMEM((NG, ROWS, 128), BF16),
            pltpu.VMEM((4, ROWS, NG * NG), BF16),
            pltpu.VMEM((NG, ROWS, 128), BF16),
            pltpu.VMEM((NG * PITCH, 128), F32),
            pltpu.VMEM((NG * PITCH, 128), F32),
            pltpu.VMEM((NG, 128), F32),
            pltpu.VMEM((NG, ROWS, 128), F32),
            pltpu.VMEM((4, 2, 8, 64, 128), BF16),
            pltpu.VMEM((4, 8, 64, 128), BF16),
            pltpu.VMEM((4, 8, 64, 128), BF16),
            pltpu.VMEM((3, 8, 64, 128), BF16),
            pltpu.VMEM((8, 64, 128), BF16),
            pltpu.VMEM((7, 64, 128), BF16),
            sems((7,)), sems((7,)), sems((3,)), sems((3,)), sems((4,)), sems((4,)), sems((4,)), sems((4,)),
            sems((4,)), sems((4,)), sems((3,)), sems((3,)), sems((7,)), sems((7,)),
        ],
        compiler_params=pltpu.CompilerParams(
            collective_id=0, has_side_effects=True, vmem_limit_bytes=48 * 2**20
        ),
    )(kpt_coord, piece, source, *tables)
    return out.reshape(2, 32, 128)[:, :27].reshape(1, 1, 2, 3456)


def solution(mesh):
    in_specs = (P("kpt", None, None, "band"), P("kpt", "band", None, None), P())
    out_specs = P("kpt", None, None, "band")
    return jax.shard_map(per_device, mesh=mesh, in_specs=in_specs, out_specs=out_specs, check_vma=False)
```

time: 842 us -> 64.3 us (0.08); the launches traced: 832 us -> 63.4 us
  waiting for transfers between devices: 332 us -> 0 us
  local copies, waits for them, and re-layouts: 286 us -> 6.42 us
  other arithmetic: 108 us -> 0 us
  Pallas kernels: 0 us -> 57 us
  blocking collectives: 47 us -> 0 us
  matrix products: 40.6 us -> 0 us
  between operations: 14.9 us -> 0.07 us
    unnamed x2 -> x0, waiting for transfers between devices: 285 us -> none
    unnamed x104 -> x13, local copies, waits for them, and re-layouts: 118 us -> 3.71 us
    another operation x56 -> x0, local copies, waits for them, and re-layouts: 83.1 us -> none
    another operation x13 -> x0, other arithmetic: 67.5 us -> none
    pallas_call x0 -> x1, Pallas kernels: none -> 57 us  [per_device(): pl.pallas_call(exchange, in_specs=[pl.BlockSpec(memory_space=pltpu.SMEM)]...]
    ppermute x7 -> x0, waiting for transfers between devices: 47.2 us -> none  [passed_along(): return lax.ppermute(block, axis, route)]
    all_gather x1 -> x0, blocking collectives: 47 us -> none  [per_device(): whole_targets = lax.all_gather(targets[0], 'band', axis=2, tiled=True)]
    dot_general x48 -> x0, matrix products: 40.6 us -> none  [transform(): jnp.einsum('pqmn,tqnc->tpcm', matrix, current, preferred_element_type=jnp...]
  transfers between devices with their start and end apart: 8 -> 0, of which waited for: 6 -> 0; matrix products, arithmetic and copies ran while one was open for 8% -> 0% of each run, Pallas kernels for 0% -> 0%
where the time goes in v1:
time: 64.3 us; the launch traced here: 63.4 us
  Pallas kernels  57 us (89%)
  local copies, waits for them, and re-layouts  6.42 us (10%)
    pallas_call x1, Pallas kernels, per_device(): pl.pallas_call(exchange, in_specs=[pl.BlockSpec(memory_space=pltpu.SMEM)]...  57 us
    unnamed x13, local copies, waits for them, and re-layouts  3.71 us
    reshape x1, local copies, waits for them, and re-layouts, per_device(): source = sources.reshape(ROWS, NG * NG)  1.33 us

profile of v1, /device:TPU:1, one launch (start us, length us, event | category | flops | bytes accessed | tf_op | source)
XLA Modules:
  0.0 63.4 jit_solution(1367736626711615551)
XLA Ops:
  0.0 0.0 copy-start.1
  0.0 0.8 %copy.11.kpt_ref = s32[8,3]{1,0:T(8,128)S(1)} copy(s32[8,3]{0,1:T(4,128)} %param.11) | data formatting | bytes 192 | tf_op args[2]
  0.8 0.7 %reshape.15 = bf16[2,27,128]{2,1,0:T(8,128)(2,1)S(1)} reshape(bf16[1,1,2,3456]{3,2,1,0:T(2,128)(2,1)} %param.9) | data formatting | bytes 27648 | tf_op jit(solution)/shard_map/reshape | solution.py:334
  1.6 0.0 copy-start.2
  1.6 0.0 copy-start.4
  1.6 1.3 %reshape.17.source_ref = bf16[96,2304]{1,0:T(8,128)(2,1)S(1)} reshape(bf16[1,1,2,110592]{3,2,1,0:T(2,128)(2,1)} %param.10) | data formatting | bytes 884736 | tf_op jit(solution)/shard_map/reshape | solution.py:335
  2.9 0.0 copy-done.1
  3.0 0.0 copy-done.2
  3.0 0.0 copy-done.4
  3.0 0.0 copy-start
  3.0 1.2 %copy-done = bf16[2,4,256,256]{3,2,1,0:T(8,128)(2,1)S(1)} copy-done((bf16[2,4,256,256]{3,2,1,0:T(8,128)(2,1)S(1)}, bf16[2,4,256,256]{3,2,1,0:T(8,128)(2,1)}, u32[]{:S(2)}) %copy-start) | copy-done | bytes 1048600
  4.2 0.0 copy-start.3
  4.2 0.9 %copy-done.3 = bf16[256,256]{1,0:T(8,128)(2,1)S(1)} copy-done((bf16[256,256]{1,0:T(8,128)(2,1)S(1)}, bf16[256,256]{1,0:T(8,128)(2,1)}, u32[]{:S(2)}) %copy-start.3) | copy-done | bytes 131096
  5.1 0.0 copy-start.5
  5.1 0.7 %copy-done.5 = bf16[96,96]{1,0:T(8,128)(2,1)S(1)} copy-done((bf16[96,96]{1,0:T(8,128)(2,1)S(1)}, bf16[96,96]{1,0:T(8,128)(2,1)}, u32[]{:S(2)}) %copy-start.5) | copy-done | bytes 18456
  5.8 57.0 %shard_map.91 = f32[64,128]{1,0:T(8,128)S(1)} custom-call(s32[8,3]{1,0:T(8,128)S(1)} %copy.11.kpt_ref, bf16[64,128]{1,0:T(8,128)(2,1)S(1)} %bitcast.4, bf16[96,2304]{1,0:T(8,128)(2,1)S(1)} %reshape.17.source_ref, bf16[96,96]{1,0:T(8,128)(2,1)S(1)} %copy-done.5, bf16[96,96]{1,0:T(8,128)(2,1)S(1)} %copy-done.4, bf16[256,256]{1,0:T(8,128)(2,1)S(1)} %copy-done.3, ...), custom_call_target="tpu_custom_call" | custom-call | tf_op jit(solution)/shard_map/pallas_call | solution.py:339
  62.8 0.6 reshape.19
  (1 shorter events, 0.0 us)
Async XLA Ops:
  0.0 2.9 %copy-start.1 = (bf16[3,512,256]{2,1,0:T(8,128)(2,1)S(1)}, bf16[3,512,256]{2,1,0:T(8,128)(2,1)}, u32[]{:S(2)}) copy-start(bf16[3,512,256]{2,1,0:T(8,128)(2,1)} %constant.20.clone.gather_ref) | copy-start | bytes 2359300
  1.6 1.4 %copy-start.2 = (bf16[256,256]{1,0:T(8,128)(2,1)S(1)}, bf16[256,256]{1,0:T(8,128)(2,1)}, u32[]{:S(2)}) copy-start(bf16[256,256]{1,0:T(8,128)(2,1)} %constant.18.clone.zbwd_ref) | copy-start | bytes 393220
  1.6 1.4 %copy-start.4 = (bf16[96,96]{1,0:T(8,128)(2,1)S(1)}, bf16[96,96]{1,0:T(8,128)(2,1)}, u32[]{:S(2)}) copy-start(bf16[96,96]{1,0:T(8,128)(2,1)} %constant.16.clone.bwd_ref) | copy-start | bytes 55300
  3.0 1.2 %copy-start = (bf16[2,4,256,256]{3,2,1,0:T(8,128)(2,1)S(1)}, bf16[2,4,256,256]{3,2,1,0:T(8,128)(2,1)}, u32[]{:S(2)}) copy-start(bf16[2,4,256,256]{3,2,1,0:T(8,128)(2,1)} %constant.19.clone.spread_ref) | copy-start | bytes 3145732
  4.2 0.9 %copy-start.3 = (bf16[256,256]{1,0:T(8,128)(2,1)S(1)}, bf16[256,256]{1,0:T(8,128)(2,1)}, u32[]{:S(2)}) copy-start(bf16[256,256]{1,0:T(8,128)(2,1)} %constant.17.clone.zfwd_ref) | copy-start | bytes 393220
  5.1 0.7 %copy-start.5 = (bf16[96,96]{1,0:T(8,128)(2,1)S(1)}, bf16[96,96]{1,0:T(8,128)(2,1)}, u32[]{:S(2)}) copy-start(bf16[96,96]{1,0:T(8,128)(2,1)} %constant.15.clone.fwd_ref) | copy-start | bytes 55300

commit v2 on v1

v2 whole, which is shorter than its diff:
```python
import functools
import math

import jax
import jax.numpy as jnp
import ml_dtypes
import numpy as np
from jax import lax
from jax.experimental import pallas as pl
from jax.experimental.pallas import tpu as pltpu
from jax.sharding import PartitionSpec as P

NG = 48
ROWS = 2 * NG
PITCH = 104
GROUP1 = 12
GROUP2 = 12
GROUP3 = 12
SPREAD_FROM = (0, 0, 128, 256)
SPREAD_WIDE = (128, 256, 256, 128)
BF16 = jnp.bfloat16
F32 = jnp.float32
MESH = pl.DeviceIdType.MESH


def host_tables():
    index = np.arange(NG)
    phases = ((index[:, None] * index[None, :]) % NG).astype(np.float32) * np.float32(2.0 * math.pi / NG)
    half_type = ml_dtypes.bfloat16
    cosine = np.cos(phases).astype(half_type).astype(np.float32)
    sine = np.sin(phases).astype(half_type).astype(np.float32)
    forward = np.block([[cosine, sine], [-sine, cosine]])
    backward = np.block([[cosine, -sine], [sine, cosine]])

    def lane_table(table):
        wide = np.zeros((2, 2, 64, 2, 2, 64), np.float32)
        for p in range(2):
            for q in range(2):
                for t in range(2):
                    wide[p, t, :NG, q, t, :NG] = table[q * NG:(q + 1) * NG, p * NG:(p + 1) * NG].T
        return wide.reshape(256, 256)

    one = np.zeros((4, 256, 2, 2, 64), np.float32)
    two = np.zeros((4, 512, 2, 2, 64), np.float32)
    gather = np.zeros((3, 4, 2, 64, 128), np.float32)
    for k in range(8):
        lanes = slice(48 * k - SPREAD_FROM[k // 2], 48 * (k + 1) - SPREAD_FROM[k // 2])
        width = SPREAD_WIDE[k // 2]
        for half in range(2):
            one[k // 2, lanes, k % 2, half, :NG] = np.eye(NG)
            two[k // 2, lanes.start + half * width:lanes.stop + half * width, k % 2, half, :NG] = np.eye(NG)
            for chunk in range(3):
                for z in range(NG):
                    lane = 48 * k + z - 128 * chunk
                    if 0 <= lane < 128:
                        gather[chunk, k - 2 * chunk, half, z, lane] = 1
    return [
        a.astype(half_type)
        for a in (
            forward,
            backward,
            lane_table(forward),
            lane_table(backward),
            one.reshape(4, 256, 256),
            two.reshape(4, 512, 256),
            gather.reshape(3, 512, 128),
        )
    ]


def dot(a, b):
    return jnp.dot(a, b, preferred_element_type=F32)


def exchange(
    kpt_hbm, slice_ref, source_ref, fwd_hbm, bwd_hbm, zfwd_hbm, zbwd_hbm, one_hbm, two_hbm, gather_hbm, out_ref,
    kpt_ref, fwd_ref, bwd_ref, zfwd_ref, zbwd_ref, one_ref, two_ref, gather_ref,
    staged, piece, slots, rows_f32, dense, targ, sources, src, work1, work2, coul, total,
    chunk_f32, chunks, passing, arrived, sums, parts, finals,
    in_sem, gz_send, gz_recv, gy_send, gy_recv, s_send, s_recv, c_send, c_recv,
    rm_send, rm_recv, ry_send, ry_recv, rz_send, rz_recv,
):
    kpt = lax.axis_index("kpt")
    band = lax.axis_index("band")
    x = kpt % 4
    y = (kpt // 4) + ((band // 2) % 2) * 2
    z = band // 4
    c = band % 2
    mine = y // 2
    primary = c == y % 2

    def device(x_, y_, z_, c_):
        return ((y_ % 2) * 4 + x_, z_ * 4 + (y_ // 2) * 2 + c_)

    def link(source, target, send, recv, where):
        return pltpu.make_async_remote_copy(
            src_ref=source, dst_ref=target, send_sem=send, recv_sem=recv, device_id=where, device_id_type=MESH
        )

    def push(*args):
        copy = link(*args)
        copy.start()
        return copy

    x_up = device((x + 1) % 4, y, z, c)
    x_down = device((x + 3) % 4, y, z, c)
    y_up = device(x, (y + 1) % 4, z, c)
    y_down = device(x, (y + 3) % 4, z, c)
    other = device(x, y, z, 1 - c)

    fetched = [
        pltpu.make_async_copy(a, b, in_sem.at[i])
        for i, (a, b) in enumerate(
            (
                (kpt_hbm, kpt_ref), (fwd_hbm, fwd_ref), (bwd_hbm, bwd_ref), (zfwd_hbm, zfwd_ref),
                (zbwd_hbm, zbwd_ref), (one_hbm, one_ref), (two_hbm, two_ref), (gather_hbm, gather_ref),
            )
        )
    ]
    for copy in fetched:
        copy.start()

    barrier = pltpu.get_barrier_semaphore()
    peers = [device(x, y, (z + d) % 8, e) for d in range(1, 8) for e in range(2)]
    for peer in [x_up, x_down, y_up, y_down, other] + peers:
        pl.semaphore_signal(barrier, inc=1, device_id=peer, device_id_type=MESH)

    for k in range(27):
        pair = slice_ref[:, 128 * k:128 * k + 128].astype(F32)
        staged[k:k + 1, :] = pair[0:1]
        staged[32 + k:33 + k, :] = pair[1:2]
    piece[...] = staged[...].astype(BF16)

    pl.semaphore_wait(barrier, 19)

    def to_primary(d):
        return link(
            piece, slots.at[mine, z, c], gz_send.at[d], gz_recv.at[d, c], device(x, y, (z + d) % 8, y % 2)
        )

    for d in range(1, 8):
        to_primary(d).start()

    @pl.when(jnp.logical_not(primary))
    def _():
        to_primary(0).start()

    low = pl.ds(0, NG)
    high = pl.ds(NG, NG)
    up_sends = [
        push(source_ref.at[part], sources.at[1, c, part], s_send.at[n], s_recv.at[n], x_up)
        for n, part in ((0, low), (2, high))
    ]
    down_sends = [
        push(source_ref.at[part], sources.at[2, c, part], s_send.at[n], s_recv.at[n], x_down)
        for n, part in ((1, high), (3, low))
    ]
    beside = push(source_ref, sources.at[0, c], c_send.at[0], c_recv.at[0], other)
    sources[0, c] = source_ref[...]

    @pl.when(primary)
    def _():
        slots[mine, z, c] = piece[...]

    total[...] = jnp.zeros_like(total)

    def across(num):
        return link(sources.at[num, c], sources.at[num, c], c_send.at[num], c_recv.at[num], other)

    def relay(n):
        part, frm, to = ((low, 1, x_up), (high, 2, x_down))[n]
        return link(
            sources.at[frm, c, part], sources.at[3, c, part], s_send.at[4 + n], s_recv.at[4 + n], to
        )

    first = pl.ds(0, 4)
    second = pl.ds(4, 4)

    def along_y(n, who, to):
        part = (first, second, second, first)[n]
        return link(slots.at[who, part], slots.at[who, part], gy_send.at[n], gy_recv.at[n], to)

    @pl.when(primary)
    def _():
        for d in range(8):
            for e in range(2):
                if d:
                    link(
                        piece, slots.at[mine, z, c], gz_send.at[d], gz_recv.at[d, e], other
                    ).wait_recv()
        link(piece, slots.at[mine, z, c], gz_send.at[0], gz_recv.at[0, 1 - c], other).wait_recv()
        for n, to in ((0, y_up), (1, y_down), (2, y_up), (3, y_down)):
            along_y(n, mine, to).start()

    up_sends[0].wait_recv()
    relay(0).start()
    down_sends[0].wait_recv()
    relay(1).start()

    @pl.when(primary)
    def _():
        along_y(0, 1 - mine, y_up).wait_recv()
        along_y(1, 1 - mine, y_down).wait_recv()
        for n, to in ((0, y_up), (1, y_down), (2, y_up), (3, y_down)):
            along_y(n, mine, to).wait_send()

    below = ((y + 3) % 4) // 2
    above = ((y + 1) % 4) // 2

    @pl.when(jnp.logical_not(primary))
    def _():
        along_y(0, below, y_up).wait_recv()
        along_y(0, below, y_up).start()
        along_y(1, above, y_down).wait_recv()
        along_y(1, above, y_down).start()
        along_y(2, below, y_up).wait_recv()
        along_y(3, above, y_down).wait_recv()
        along_y(0, below, y_up).wait_send()
        along_y(1, above, y_down).wait_send()

    def unpack(z_, carry):
        for h in range(2):
            for e in range(2):
                got = slots[h, z_, e].astype(F32)
                for p in range(2):
                    rows_f32[pl.ds(p * 864 + 108 * z_ + 54 * h + 27 * e, 27), :] = got[p * 32:p * 32 + 27]
        return carry

    lax.fori_loop(0, 8, unpack, 0)
    for p in range(2):
        for col in range(18):
            dense[p * NG:(p + 1) * NG, col * 128:(col + 1) * 128] = rows_f32[
                pl.ds(p * 864 + col, NG, stride=18), :
            ].astype(BF16)

    for copy in fetched:
        copy.wait()

    def spread_out(read, table, copies, store):
        for g in range(6):
            for k in range(4):
                width = SPREAD_WIDE[k]
                lanes = slice(384 * g + SPREAD_FROM[k], 384 * g + SPREAD_FROM[k] + width)
                rows = [read(i, lanes) for i in range(copies)]
                wide = dot(rows[0] if copies == 1 else jnp.concatenate(rows, axis=1), table[k, :copies * width, :])
                wide = wide.astype(BF16)
                store[8 * g + 2 * k] = wide[:, :128]
                store[8 * g + 2 * k + 1] = wide[:, 128:]

    spread_out(lambda i, lanes: dense[:, lanes], one_ref, 1, targ)

    up_sends[1].wait_recv()
    across(1).start()

    lane = lax.broadcasted_iota(jnp.int32, (NG, 128), 1)
    row = lax.broadcasted_iota(jnp.int32, (NG, 128), 0)

    def frequency(i):
        return jnp.where(i < NG // 2, i, i - NG).astype(F32)

    scale = 4.0 * math.pi / float(NG**3)
    forward = fwd_ref[...]
    backward = bwd_ref[...]
    zforward = zfwd_ref[...]
    zbackward = zbwd_ref[...]

    def step(num, carry):
        @pl.when(num == 1)
        def _():
            down_sends[1].wait_recv()
            across(2).start()

        @pl.when(num == 2)
        def _():
            relay(0).wait_recv()
            relay(1).wait_recv()
            across(3).start()

        across(num).wait_recv()
        spread_out(lambda i, lanes: sources[num, i, :, lanes], two_ref, 2, src)
        from_x = jnp.where(num == 0, 0, jnp.where(num == 1, 3, jnp.where(num == 2, 1, 2)))
        from_k = (kpt // 4) * 4 + (x + from_x) % 4

        def offset(d):
            return (kpt_ref[c * 4 + x, d] - kpt_ref[from_k, d]).astype(F32) * 0.25

        fx = frequency(row) + offset(0)
        fy = frequency(row) + offset(1)
        fz = frequency(lane % 64) + offset(2)
        coul[...] = 0.04 * (fx * fx)
        fyz = 0.04 * (fy * fy + fz * fz) + 0.25

        def into_spectrum(i, carry):
            mixed = []
            for j in range(GROUP1):
                pair = []
                for cell in (2 * (i * GROUP1 + j), 2 * (i * GROUP1 + j) + 1):
                    s = src[cell].astype(F32)
                    t = targ[cell].astype(F32)
                    sr, si, tr, ti = s[:NG], s[NG:], t[:NG], t[NG:]
                    pair.append(
                        jnp.concatenate([(sr * tr + si * ti).astype(BF16), (sr * ti - si * tr).astype(BF16)], axis=0)
                    )
                after_x = dot(forward, jnp.concatenate(pair, axis=1)).astype(BF16)
                for h in (0, 128):
                    mixed.append(jnp.concatenate([after_x[:NG, h:h + 128], after_x[NG:, h:h + 128]], axis=1))
            after_z = dot(jnp.concatenate(mixed, axis=0), zforward)
            for j in range(2 * GROUP1):
                for p in range(2):
                    start = (2 * i * GROUP1 + j) * PITCH + p * NG
                    work1[pl.ds(start, NG), :] = after_z[j * NG:(j + 1) * NG, p * 128:p * 128 + 128]
            return carry

        def through_spectrum(i, carry):
            for j in range(GROUP2):
                cells = (2 * (i * GROUP2 + j), 2 * (i * GROUP2 + j) + 1)
                pair = [
                    jnp.concatenate(
                        [work1[pl.ds(cell + p * NG, NG, stride=PITCH), :].astype(BF16) for p in range(2)], axis=0
                    )
                    for cell in cells
                ]
                spectrum = dot(forward, jnp.concatenate(pair, axis=1))
                pair = []
                for h, cell in enumerate(cells):
                    factor = scale / (fyz + coul[pl.ds(cell, 1), :])
                    part = spectrum[:, h * 128:h * 128 + 128]
                    pair.append(
                        jnp.concatenate([(part[:NG] * factor).astype(BF16), (part[NG:] * factor).astype(BF16)], axis=0)
                    )
                after_y = dot(backward, jnp.concatenate(pair, axis=1))
                for h, cell in enumerate(cells):
                    work2[pl.ds(cell * PITCH, ROWS), :] = after_y[:, h * 128:h * 128 + 128]
            return carry

        def out_of_spectrum(i, carry):
            mixed = [
                jnp.concatenate(
                    [
                        work2[pl.ds(2 * i * GROUP3 + j + p * NG, NG, stride=PITCH), :].astype(BF16)
                        for p in range(2)
                    ],
                    axis=1,
                )
                for j in range(2 * GROUP3)
            ]
            after_z = dot(jnp.concatenate(mixed, axis=0), zbackward).astype(BF16)
            for j in range(GROUP3):
                pair = [
                    jnp.concatenate([after_z[n * NG:(n + 1) * NG, :128], after_z[n * NG:(n + 1) * NG, 128:]], axis=0)
                    for n in (2 * j, 2 * j + 1)
                ]
                potential = dot(backward, jnp.concatenate(pair, axis=1))
                for h in range(2):
                    cell = 2 * (i * GROUP3 + j) + h
                    s = src[cell].astype(F32)
                    sr, si = s[:NG], s[NG:]
                    pr = potential[:NG, h * 128:h * 128 + 128]
                    pi = potential[NG:, h * 128:h * 128 + 128]
                    total[cell, :NG, :] += sr * pr - si * pi
                    total[cell, NG:, :] += sr * pi + si * pr
            return carry

        lax.fori_loop(0, 24 // GROUP1, into_spectrum, 0)
        lax.fori_loop(0, 24 // GROUP2, through_spectrum, 0)
        lax.fori_loop(0, 24 // GROUP3, out_of_spectrum, 0)
        return carry

    lax.fori_loop(0, 4, step, 0)

    for g in range(6):
        for chunk in range(3):
            cells = [8 * g + 2 * chunk + k for k in range(4)]
            narrow = dot(jnp.concatenate([total[n].astype(BF16) for n in cells], axis=1), gather_ref[chunk])
            for p in range(2):
                rows_f32[pl.ds(p * 864 + 3 * g + chunk, NG, stride=18), :] = narrow[p * NG:(p + 1) * NG]

    def pack(z_, carry):
        for h in range(2):
            for p in range(2):
                chunk_f32[h, p, pl.ds(54 * z_, 54), :] = rows_f32[pl.ds(p * 864 + 108 * z_ + 54 * h, 54), :]
        return carry

    lax.fori_loop(0, 8, pack, 0)
    chunks[...] = chunk_f32[:, :, :432, :].astype(BF16)

    def middle(n):
        return link(
            chunks.at[1 - mine, n], passing.at[n], rm_send.at[n], rm_recv.at[n], (y_down, y_up)[n]
        )

    def onward(n, p, buffer):
        return link(buffer, arrived.at[n, p], ry_send.at[n, p], ry_recv.at[n, p], (y_up, y_down)[n])

    @pl.when(primary)
    def _():
        middle(0).start()
        middle(1).start()

    @pl.when(jnp.logical_not(primary))
    def _():
        onward(0, 0, chunks.at[above, 0]).start()
        onward(1, 1, chunks.at[below, 1]).start()
        middle(0).wait_recv()
        chunks[below, 0] = (chunks[below, 0].astype(F32) + passing[0].astype(F32)).astype(BF16)
        onward(1, 0, chunks.at[below, 0]).start()
        middle(1).wait_recv()
        chunks[above, 1] = (chunks[above, 1].astype(F32) + passing[1].astype(F32)).astype(BF16)
        onward(0, 1, chunks.at[above, 1]).start()

    def share(d, e):
        return link(
            parts.at[(z + d) % 8, e], finals.at[d], rz_send.at[d, e], rz_recv.at[d], device(x, y, (z + d) % 8, e)
        )

    @pl.when(primary)
    def _():
        for p in range(2):
            onward(0, p, chunks.at[0, p]).wait_recv()
            onward(1, p, chunks.at[0, p]).wait_recv()
            sums[p, :432, :] = (
                chunks[mine, p].astype(F32) + arrived[0, p].astype(F32) + arrived[1, p].astype(F32)
            )

        def split(z_, carry):
            for e in range(2):
                for p in range(2):
                    parts[z_, e, p * 32:p * 32 + 32, :] = sums[p, pl.ds(54 * z_ + 27 * e, 32), :].astype(BF16)
            return carry

        lax.fori_loop(0, 8, split, 0)
        for d in range(1, 8):
            for e in range(2):
                share(d, e).start()
        share(0, 1 - c).start()
        finals[0] = parts[z, c]

    @pl.when(jnp.logical_not(primary))
    def _():
        share(0, c).wait_recv()

    for d in range(1, 8):
        share(d, c).wait_recv()
    result = sum([finals[d].astype(F32) for d in range(1, 8)], finals[0].astype(F32)) * (-1.0 / 8.0)
    for k in range(27):
        for p in range(2):
            out_ref[p:p + 1, 128 * k:128 * k + 128] = result[p * 32 + k:p * 32 + k + 1]

    for d in range(1, 8):
        to_primary(d).wait_send()
    for copy in up_sends + down_sends + [across(n) for n in range(4)] + [relay(0), relay(1)]:
        copy.wait_send()

    @pl.when(primary)
    def _():
        for n in range(2):
            middle(n).wait_send()
        for d in range(1, 8):
            for e in range(2):
                share(d, e).wait_send()
        share(0, 1 - c).wait_send()

    @pl.when(jnp.logical_not(primary))
    def _():
        to_primary(0).wait_send()
        for n in range(2):
            for p in range(2):
                onward(n, p, chunks.at[0, p]).wait_send()


def per_device(targets, sources, kpt_coord):
    tables = [jnp.asarray(a) for a in host_tables()]
    vmem = pl.BlockSpec(memory_space=pltpu.VMEM)
    anywhere = pl.BlockSpec(memory_space=pl.ANY)
    sems = pltpu.SemaphoreType.DMA
    out = pl.pallas_call(
        exchange,
        in_specs=[anywhere, vmem, vmem] + [anywhere] * 7,
        out_specs=vmem,
        out_shape=jax.ShapeDtypeStruct((2, 3456), F32),
        scratch_shapes=[pltpu.SMEM((8, 3), jnp.int32)]
        + [pltpu.VMEM(a.shape, BF16) for a in tables]
        + [
            pltpu.VMEM((64, 128), F32),
            pltpu.VMEM((64, 128), BF16),
            pltpu.VMEM((2, 8, 2, 64, 128), BF16),
            pltpu.VMEM((1736, 128), F32),
            pltpu.VMEM((ROWS, NG * NG), BF16),
            pltpu.VMEM((NG, ROWS, 128), BF16),
            pltpu.VMEM((4, 2, ROWS, NG * NG), BF16),
            pltpu.VMEM((NG, ROWS, 128), BF16),
            pltpu.VMEM((NG * PITCH, 128), F32),
            pltpu.VMEM((NG * PITCH, 128), F32),
            pltpu.VMEM((NG, 128), F32),
            pltpu.VMEM((NG, ROWS, 128), F32),
            pltpu.VMEM((2, 2, 440, 128), F32),
            pltpu.VMEM((2, 2, 432, 128), BF16),
            pltpu.VMEM((2, 432, 128), BF16),
            pltpu.VMEM((2, 2, 432, 128), BF16),
            pltpu.VMEM((2, 440, 128), F32),
            pltpu.VMEM((8, 2, 64, 128), BF16),
            pltpu.VMEM((8, 64, 128), BF16),
            sems((8,)), sems((8,)), sems((8, 2)), sems((4,)), sems((4,)), sems((6,)), sems((6,)),
            sems((4,)), sems((4,)), sems((2,)), sems((2,)), sems((2, 2)), sems((2, 2)), sems((8, 2)), sems((8,)),
        ],
        compiler_params=pltpu.CompilerParams(
            collective_id=0, has_side_effects=True, vmem_limit_bytes=48 * 2**20
        ),
    )(kpt_coord, targets.reshape(2, 3456), sources.reshape(ROWS, NG * NG), *tables)
    return out.reshape(1, 1, 2, 3456)


def solution(mesh):
    in_specs = (P("kpt", None, None, "band"), P("kpt", "band", None, None), P())
    out_specs = P("kpt", None, None, "band")
    return jax.shard_map(per_device, mesh=mesh, in_specs=in_specs, out_specs=out_specs, check_vma=False)
```

time: 64.3 us -> 66.4 us (1.033); the launches traced: 63.4 us -> 66.2 us
  Pallas kernels: 57 us -> 61.1 us
  local copies, waits for them, and re-layouts: 6.42 us -> 5 us
    pallas_call x1, Pallas kernels: 57 us -> 61.1 us  [per_device(): pl.pallas_call(exchange, in_specs=[anywhere, vmem, vmem] + [anywhere] * 7...]
    reshape x3 -> x1, local copies, waits for them, and re-layouts: 2.7 us -> 1.33 us  [per_device(): sources.reshape(ROWS, NG * NG)]
    unnamed x13 -> x18, local copies, waits for them, and re-layouts: 3.71 us -> 3.67 us
where the time goes in v2:
time: 66.4 us; the launch traced here: 66.2 us
  Pallas kernels  61.1 us (92%)
  local copies, waits for them, and re-layouts  5 us (8%)
    pallas_call x1, Pallas kernels, per_device(): pl.pallas_call(exchange, in_specs=[anywhere, vmem, vmem] + [anywhere] * 7...  61.1 us
    unnamed x18, local copies, waits for them, and re-layouts  3.67 us
    reshape x1, local copies, waits for them, and re-layouts, per_device(): sources.reshape(ROWS, NG * NG)  1.33 us

profile of v2, /device:TPU:1, one launch (start us, length us, event | category | flops | bytes accessed | tf_op | source)
XLA Modules:
  0.0 66.2 jit_solution(9593368068157114447)
XLA Ops:
  0.0 0.0 copy-start.1
  0.0 0.8 %copy.11.kpt_hbm = s32[8,3]{1,0:T(8,128)S(1)} copy(s32[8,3]{0,1:T(4,128)} %param.12) | data formatting | bytes 192 | tf_op args[2]
  0.8 0.0 copy-start.3
  0.8 0.0 copy-start.4
  0.8 0.0 copy-start.5
  0.8 0.0 copy-start.6
  0.8 0.0 copy-start.7
  0.8 1.3 %reshape.10.source_ref = bf16[96,2304]{1,0:T(8,128)(2,1)S(1)} reshape(bf16[1,1,2,110592]{3,2,1,0:T(2,128)(2,1)} %param.11) | data formatting | bytes 884736 | tf_op jit(solution)/shard_map/reshape | solution.py:509
  2.2 0.0 copy-done.1
  2.2 0.0 copy-done.3
  2.2 0.0 copy-done.4
  2.2 0.0 copy-done.5
  2.2 0.0 copy-done.6
  2.2 0.0 copy-done.7
  2.2 0.0 copy-start
  2.3 1.2 %copy-done = bf16[4,512,256]{2,1,0:T(8,128)(2,1)S(1)} copy-done((bf16[4,512,256]{2,1,0:T(8,128)(2,1)S(1)}, bf16[4,512,256]{2,1,0:T(8,128)(2,1)}, u32[]{:S(2)}) %copy-start) | copy-done | bytes 1048600
  3.5 0.0 copy-start.2
  3.5 1.0 %copy-done.2 = bf16[3,512,128]{2,1,0:T(8,128)(2,1)S(1)} copy-done((bf16[3,512,128]{2,1,0:T(8,128)(2,1)S(1)}, bf16[3,512,128]{2,1,0:T(8,128)(2,1)}, u32[]{:S(2)}) %copy-start.2) | copy-done | bytes 393240
  4.5 61.1 %shard_map.100 = f32[2,3456]{1,0:T(2,128)S(1)} custom-call(s32[8,3]{1,0:T(8,128)S(1)} %copy.11.kpt_hbm, bf16[2,3456]{1,0:T(2,128)(2,1)S(1)} %bitcast.3, bf16[96,2304]{1,0:T(8,128)(2,1)S(1)} %reshape.10.source_ref, bf16[96,96]{1,0:T(8,128)(2,1)S(1)} %copy-done.6, bf16[96,96]{1,0:T(8,128)(2,1)S(1)} %copy-done.5, bf16[256,256]{1,0:T(8,128)(2,1)S(1)} %copy-done.4, ...), custom_call_target="tpu_custom_call" | custom-call | tf_op jit(solution)/shard_map/pallas_call | solution.py:476
  65.6 0.6 copy.13
Async XLA Ops:
  0.0 2.2 %copy-start.1 = (bf16[4,256,256]{2,1,0:T(8,128)(2,1)S(1)}, bf16[4,256,256]{2,1,0:T(8,128)(2,1)}, u32[]{:S(2)}) copy-start(bf16[4,256,256]{2,1,0:T(8,128)(2,1)} %constant.18.clone.one_hbm) | copy-start | bytes 1572868
  0.8 1.4 %copy-start.3 = (bf16[256,256]{1,0:T(8,128)(2,1)S(1)}, bf16[256,256]{1,0:T(8,128)(2,1)}, u32[]{:S(2)}) copy-start(bf16[256,256]{1,0:T(8,128)(2,1)} %constant.17.clone.zbwd_hbm) | copy-start | bytes 393220
  0.8 1.4 %copy-start.4 = (bf16[256,256]{1,0:T(8,128)(2,1)S(1)}, bf16[256,256]{1,0:T(8,128)(2,1)}, u32[]{:S(2)}) copy-start(bf16[256,256]{1,0:T(8,128)(2,1)} %constant.16.clone.zfwd_hbm) | copy-start | bytes 393220
  0.8 1.4 %copy-start.5 = (bf16[96,96]{1,0:T(8,128)(2,1)S(1)}, bf16[96,96]{1,0:T(8,128)(2,1)}, u32[]{:S(2)}) copy-start(bf16[96,96]{1,0:T(8,128)(2,1)} %constant.15.clone.bwd_hbm) | copy-start | bytes 55300
  0.8 1.4 %copy-start.6 = (bf16[96,96]{1,0:T(8,128)(2,1)S(1)}, bf16[96,96]{1,0:T(8,128)(2,1)}, u32[]{:S(2)}) copy-start(bf16[96,96]{1,0:T(8,128)(2,1)} %constant.14.clone.fwd_hbm) | copy-start | bytes 55300
  0.8 1.4 %copy-start.7 = (bf16[1,1,2,3456]{3,2,1,0:T(2,128)(2,1)S(1)}, bf16[1,1,2,3456]{3,2,1,0:T(2,128)(2,1)}, u32[]{:S(2)}) copy-start(bf16[1,1,2,3456]{3,2,1,0:T(2,128)(2,1)} %param.10) | copy-start | bytes 41476
  2.2 1.2 %copy-start = (bf16[4,512,256]{2,1,0:T(8,128)(2,1)S(1)}, bf16[4,512,256]{2,1,0:T(8,128)(2,1)}, u32[]{:S(2)}) copy-start(bf16[4,512,256]{2,1,0:T(8,128)(2,1)} %constant.19.clone.two_hbm) | copy-start | bytes 3145732
  3.5 1.0 %copy-start.2 = (bf16[3,512,128]{2,1,0:T(8,128)(2,1)S(1)}, bf16[3,512,128]{2,1,0:T(8,128)(2,1)}, u32[]{:S(2)}) copy-start(bf16[3,512,128]{2,1,0:T(8,128)(2,1)} %constant.20.clone.gather_hbm) | copy-start | bytes 1179652

commit v3 on v0

v3 whole, which is shorter than its diff:
```python
import functools
import math

import jax
import jax.numpy as jnp
import ml_dtypes
import numpy as np
from jax import lax
from jax.experimental import pallas as pl
from jax.experimental.pallas import tpu as pltpu
from jax.sharding import PartitionSpec as P

NG = 48
ROWS = 2 * NG
PITCH = 104
GROUP1 = 24
GROUP2 = 24
GROUP3 = 24
BATCH = 2
SPAN = NG * PITCH
SPREAD_FROM = (0, 0, 128, 256)
SPREAD_WIDE = (128, 256, 256, 128)
BF16 = jnp.bfloat16
F32 = jnp.float32
MESH = pl.DeviceIdType.MESH


def host_tables():
    index = np.arange(NG)
    phases = ((index[:, None] * index[None, :]) % NG).astype(np.float32) * np.float32(2.0 * math.pi / NG)
    half_type = ml_dtypes.bfloat16
    cosine = np.cos(phases).astype(half_type).astype(np.float32)
    sine = np.sin(phases).astype(half_type).astype(np.float32)
    forward = np.block([[cosine, sine], [-sine, cosine]])
    backward = np.block([[cosine, -sine], [sine, cosine]])

    def lane_table(table):
        wide = np.zeros((2, 2, 64, 2, 2, 64), np.float32)
        for p in range(2):
            for q in range(2):
                for t in range(2):
                    wide[p, t, :NG, q, t, :NG] = table[q * NG:(q + 1) * NG, p * NG:(p + 1) * NG].T
        return wide.reshape(256, 256)

    one = np.zeros((4, 256, 2, 2, 64), np.float32)
    two = np.zeros((4, 512, 2, 2, 64), np.float32)
    gather = np.zeros((3, 4, 2, 64, 128), np.float32)
    for k in range(8):
        lanes = slice(48 * k - SPREAD_FROM[k // 2], 48 * (k + 1) - SPREAD_FROM[k // 2])
        width = SPREAD_WIDE[k // 2]
        for half in range(2):
            one[k // 2, lanes, k % 2, half, :NG] = np.eye(NG)
            two[k // 2, lanes.start + half * width:lanes.stop + half * width, k % 2, half, :NG] = np.eye(NG)
            for chunk in range(3):
                for z in range(NG):
                    lane = 48 * k + z - 128 * chunk
                    if 0 <= lane < 128:
                        gather[chunk, k - 2 * chunk, half, z, lane] = 1
    return [
        a.astype(half_type)
        for a in (
            forward,
            backward,
            lane_table(forward),
            lane_table(backward),
            one.reshape(4, 256, 256),
            two.reshape(4, 512, 256),
            gather.reshape(3, 512, 128),
        )
    ]


def dot(a, b):
    return jnp.dot(a, b, preferred_element_type=F32)


def exchange(
    kpt_hbm, slice_hbm, source_hbm, fwd_hbm, bwd_hbm, zfwd_hbm, zbwd_hbm, one_hbm, two_hbm, gather_hbm, out_ref,
    kpt_ref, slice_ref, raw_ref, fwd_ref, bwd_ref, zfwd_ref, zbwd_ref, one_ref, two_ref, gather_ref,
    staged, piece, carried, slots, rows_f32, dense, targ, sources, src, work1, work2, coul, base, total,
    chunks, arrived, parts, finals,
    in_sem, gz_send, gz_recv, gy_send, gy_recv, s_send, s_recv, c_send, c_recv,
    ry_send, ry_recv, rz_send, rz_recv,
):
    kpt = lax.axis_index("kpt")
    band = lax.axis_index("band")
    x = kpt % 4
    y = (kpt // 4) + ((band // 2) % 2) * 2
    z = band // 4
    c = band % 2
    mine = y // 2
    primary = c == y % 2
    secondary = c != y % 2

    def device(x_, y_, z_, c_):
        return ((y_ % 2) * 4 + x_, z_ * 4 + (y_ // 2) * 2 + c_)

    def link(source, target, send, recv, where):
        return pltpu.make_async_remote_copy(
            src_ref=source, dst_ref=target, send_sem=send, recv_sem=recv, device_id=where, device_id_type=MESH
        )

    x_up = device((x + 1) % 4, y, z, c)
    x_down = device((x + 3) % 4, y, z, c)
    other = device(x, y, z, 1 - c)

    fetched = [
        pltpu.make_async_copy(a, b, in_sem.at[i])
        for i, (a, b) in enumerate(
            (
                (slice_hbm, slice_ref), (source_hbm, raw_ref), (kpt_hbm, kpt_ref), (one_hbm, one_ref),
                (two_hbm, two_ref), (fwd_hbm, fwd_ref), (bwd_hbm, bwd_ref), (zfwd_hbm, zfwd_ref),
                (zbwd_hbm, zbwd_ref), (gather_hbm, gather_ref),
            )
        )
    ]
    for copy in fetched:
        copy.start()

    barrier = pltpu.get_barrier_semaphore()
    peers = [x_up, x_down, other] + [device(x, y, (z + d) % 8, c) for d in range(1, 8)]
    peers += [device(x, (y + d) % 4, z, e) for d in range(1, 4) for e in range(2)]
    for peer in peers:
        pl.semaphore_signal(barrier, inc=1, device_id=peer, device_id_type=MESH)

    fetched[0].wait()
    for k in range(27):
        staged[2 * k:2 * k + 2, :] = slice_ref[:, 128 * k:128 * k + 128].astype(F32)
    piece[...] = staged[...].astype(BF16)

    pl.semaphore_wait(barrier, len(peers))

    def along_z(d):
        return link(piece, carried.at[z], gz_send.at[d], gz_recv.at[d], device(x, y, (z + d) % 8, c))

    def along_y(d, held, z_):
        return link(
            held, slots.at[mine, c, z_], gy_send.at[d], gy_recv.at[d, c], device(x, (y + d) % 4, z, y % 2)
        )

    def spread_y(held, z_):
        for d in range(1, 4):
            along_y(d, held, z_).start()

        @pl.when(secondary)
        def _():
            along_y(0, held, z_).start()

    for d in (4, 3, 5, 2, 6, 1, 7):
        along_z(d).start()
    spread_y(piece, z)

    fetched[1].wait()

    def densify(raw, store):
        for p in range(2):
            for col in range(18):
                store(p, col, raw[pl.ds(2 * col + p, NG, stride=36), :].astype(BF16))

    rows_f32[pl.ds(0, 2 * 864), :] = raw_ref[...].astype(F32)

    def keep_source(p, col, block):
        sources[0, c, p * NG:(p + 1) * NG, col * 128:(col + 1) * 128] = block

    densify(rows_f32, keep_source)

    low = pl.ds(0, NG)
    high = pl.ds(NG, NG)
    legs = ((low, 1, x_up), (high, 2, x_down), (high, 1, x_up), (low, 2, x_down))

    def along_x(n):
        part, place, to = legs[n]
        return link(sources.at[0, c, part], sources.at[place, c, part], s_send.at[n], s_recv.at[n], to)

    def relay(n):
        part, place, to = legs[n]
        return link(sources.at[place, c, part], sources.at[3, c, part], s_send.at[4 + n], s_recv.at[4 + n], to)

    def across(num):
        return link(sources.at[num, c], sources.at[num, c], c_send.at[num], c_recv.at[num], other)

    for n in range(4):
        along_x(n).start()
    across(0).start()
    total[...] = jnp.zeros_like(total)

    for d in (1, 7, 2, 6, 3, 5, 4):
        along_z(d).wait_recv()
        from_z = (z + 8 - d) % 8
        spread_y(carried.at[from_z], from_z)

    along_x(0).wait_recv()
    relay(0).start()
    along_x(1).wait_recv()
    relay(1).start()

    def group(d, h, e):
        whole = slots.at[h, e]
        return link(whole, whole, gy_send.at[d], gy_recv.at[d, e], other)

    @pl.when(primary)
    def _():
        carried[z] = piece[...]
        slots[mine, c] = carried[...]
        group(0, mine, 1 - c).wait_recv()
        for e in range(2):
            group(2, 1 - mine, e).wait_recv()

    @pl.when(secondary)
    def _():
        for e in range(2):
            group(1, ((y + 3) % 4) // 2, e).wait_recv()
            group(3, ((y + 1) % 4) // 2, e).wait_recv()

    def unpack(z_, carry):
        for h in range(2):
            for e in range(2):
                start = 54 * (4 * z_ + 2 * h + e)
                rows_f32[pl.ds(start, 54), :] = slots[h, e, z_].astype(F32)[:54]
        return carry

    lax.fori_loop(0, 8, unpack, 0)

    def keep_target(p, col, block):
        dense[p * NG:(p + 1) * NG, col * 128:(col + 1) * 128] = block

    densify(rows_f32, keep_target)

    for copy in fetched[2:]:
        copy.wait()

    def spread_out(read, table, copies, store):
        for g in range(6):
            for k in range(4):
                width = SPREAD_WIDE[k]
                lanes = slice(384 * g + SPREAD_FROM[k], 384 * g + SPREAD_FROM[k] + width)
                rows = [read(i, lanes) for i in range(copies)]
                wide = dot(rows[0] if copies == 1 else jnp.concatenate(rows, axis=1), table[k, :copies * width, :])
                wide = wide.astype(BF16)
                store(8 * g + 2 * k, wide[:, :128])
                store(8 * g + 2 * k + 1, wide[:, 128:])

    def set_target(cell, block):
        targ[cell] = block

    spread_out(lambda i, lanes: dense[:, lanes], one_ref, 1, set_target)

    along_x(2).wait_recv()
    across(1).start()

    lane = lax.broadcasted_iota(jnp.int32, (NG, 128), 1)
    row = lax.broadcasted_iota(jnp.int32, (NG, 128), 0)

    def frequency(i):
        return jnp.where(i < NG // 2, i, i - NG).astype(F32)

    scale = 4.0 * math.pi / float(NG**3)
    forward = fwd_ref[...]
    backward = bwd_ref[...]
    zforward = zfwd_ref[...]
    zbackward = zbwd_ref[...]

    def prepare(num, carry):
        @pl.when(num == 2)
        def _():
            along_x(3).wait_recv()
            across(2).start()
            relay(0).wait_recv()
            relay(1).wait_recv()
            across(3).start()

        across(num).wait_recv()
        at = num % BATCH

        def set_source(cell, block):
            src[at, cell] = block

        spread_out(lambda i, lanes: sources[num, i, :, lanes], two_ref, 2, set_source)
        from_x = jnp.where(num == 0, 0, jnp.where(num == 1, 3, jnp.where(num == 2, 1, 2)))
        from_k = (kpt // 4) * 4 + (x + from_x) % 4

        def offset(d):
            return (kpt_ref[d, c * 4 + x] - kpt_ref[d, from_k]).astype(F32) * 0.25

        fx = frequency(row) + offset(0)
        fy = frequency(row) + offset(1)
        fz = frequency(lane % 64) + offset(2)
        coul[at] = 0.04 * (fx * fx)
        base[at] = 0.04 * (fy * fy + fz * fz) + 0.25
        return carry

    def into_spectrum(at, i):
        mixed = []
        for j in range(GROUP1):
            pair = []
            for cell in (2 * (i * GROUP1 + j), 2 * (i * GROUP1 + j) + 1):
                s = src[at, cell].astype(F32)
                t = targ[cell].astype(F32)
                sr, si, tr, ti = s[:NG], s[NG:], t[:NG], t[NG:]
                pair.append(
                    jnp.concatenate([(sr * tr + si * ti).astype(BF16), (sr * ti - si * tr).astype(BF16)], axis=0)
                )
            after_x = dot(forward, jnp.concatenate(pair, axis=1)).astype(BF16)
            for h in (0, 128):
                mixed.append(jnp.concatenate([after_x[:NG, h:h + 128], after_x[NG:, h:h + 128]], axis=1))
        after_z = dot(jnp.concatenate(mixed, axis=0), zforward)
        for j in range(2 * GROUP1):
            for p in range(2):
                start = at * SPAN + (2 * i * GROUP1 + j) * PITCH + p * NG
                work1[pl.ds(start, NG), :] = after_z[j * NG:(j + 1) * NG, p * 128:p * 128 + 128]

    def through_spectrum(at, i):
        for j in range(GROUP2):
            cells = (2 * (i * GROUP2 + j), 2 * (i * GROUP2 + j) + 1)
            pair = [
                jnp.concatenate(
                    [
                        work1[pl.ds(at * SPAN + cell + p * NG, NG, stride=PITCH), :].astype(BF16)
                        for p in range(2)
                    ],
                    axis=0,
                )
                for cell in cells
            ]
            spectrum = dot(forward, jnp.concatenate(pair, axis=1))
            pair = []
            for h, cell in enumerate(cells):
                factor = scale / (base[at] + coul[at, pl.ds(cell, 1), :])
                part = spectrum[:, h * 128:h * 128 + 128]
                pair.append(
                    jnp.concatenate([(part[:NG] * factor).astype(BF16), (part[NG:] * factor).astype(BF16)], axis=0)
                )
            after_y = dot(backward, jnp.concatenate(pair, axis=1))
            for h, cell in enumerate(cells):
                work2[pl.ds(at * SPAN + cell * PITCH, ROWS), :] = after_y[:, h * 128:h * 128 + 128]

    def out_of_spectrum(at, i):
        mixed = [
            jnp.concatenate(
                [
                    work2[pl.ds(at * SPAN + 2 * i * GROUP3 + j + p * NG, NG, stride=PITCH), :].astype(BF16)
                    for p in range(2)
                ],
                axis=1,
            )
            for j in range(2 * GROUP3)
        ]
        after_z = dot(jnp.concatenate(mixed, axis=0), zbackward).astype(BF16)
        for j in range(GROUP3):
            pair = [
                jnp.concatenate([after_z[n * NG:(n + 1) * NG, :128], after_z[n * NG:(n + 1) * NG, 128:]], axis=0)
                for n in (2 * j, 2 * j + 1)
            ]
            potential = dot(backward, jnp.concatenate(pair, axis=1))
            for h in range(2):
                cell = 2 * (i * GROUP3 + j) + h
                s = src[at, cell].astype(F32)
                sr, si = s[:NG], s[NG:]
                pr = potential[:NG, h * 128:h * 128 + 128]
                pi = potential[NG:, h * 128:h * 128 + 128]
                total[cell, :NG, :] += sr * pr - si * pi
                total[cell, NG:, :] += sr * pi + si * pr

    def batch(num, carry):
        lax.fori_loop(num * BATCH, num * BATCH + BATCH, prepare, 0)
        for phase, size in ((into_spectrum, GROUP1), (through_spectrum, GROUP2), (out_of_spectrum, GROUP3)):
            count = NG // 2 // size

            def one(k, carry):
                phase(k // count, k % count)
                return carry

            lax.fori_loop(0, BATCH * count, one, 0)
        return carry

    lax.fori_loop(0, 4 // BATCH, batch, 0)

    for g in range(6):
        for chunk in range(3):
            cells = [8 * g + 2 * chunk + k for k in range(4)]
            narrow = dot(jnp.concatenate([total[n].astype(BF16) for n in cells], axis=1), gather_ref[chunk])
            for p in range(2):
                rows_f32[pl.ds(2 * (3 * g + chunk) + p, NG, stride=36), :] = narrow[p * NG:(p + 1) * NG]

    def to_owner(h, e, z_, k):
        where = device(x, (y + k) % 4, z, e)
        return link(chunks.at[h, e, z_], arrived.at[z_, k], ry_send.at[h, e], ry_recv.at[z_], where)

    order = (4, 3, 5, 2, 6, 1, 7, 0)
    for d in order:
        z_ = (z + d) % 8
        for h in range(2):
            for e in range(2):
                start = 54 * (4 * z_ + 2 * h + e)
                chunks[h, e, z_] = rows_f32[pl.ds(start, 64), :].astype(BF16)

        @pl.when(primary)
        def _():
            to_owner(mine, 1 - c, z_, 0).start()
            for e in range(2):
                to_owner(1 - mine, e, z_, 2).start()
            arrived[z_, 0] = chunks[mine, c, z_]

        @pl.when(secondary)
        def _():
            for e in range(2):
                to_owner(((y + 1) % 4) // 2, e, z_, 1).start()
                to_owner(((y + 3) % 4) // 2, e, z_, 3).start()

    def share(d):
        to_z = (z + d) % 8
        return link(parts.at[to_z], finals.at[d], rz_send.at[d], rz_recv.at[d], device(x, y, to_z, c))

    for d in order:
        z_ = (z + d) % 8

        @pl.when(primary)
        def _():
            three = arrived.at[z_, pl.ds(1, 3)]
            link(three, three, ry_send.at[0, 0], ry_recv.at[z_], other).wait_recv()

        @pl.when(secondary)
        def _():
            link(arrived.at[z_], arrived.at[z_], ry_send.at[0, 0], ry_recv.at[z_], other).wait_recv()

        summed = sum([arrived[z_, k].astype(F32) for k in range(1, 4)], arrived[z_, 0].astype(F32))
        if d:
            parts[z_] = summed.astype(BF16)
            share(d).start()

    for d in range(1, 8):
        share(d).wait_recv()
        summed = summed + finals[d].astype(F32)
    result = summed * (-1.0 / 8.0)
    for k in range(27):
        out_ref[:, 128 * k:128 * k + 128] = result[2 * k:2 * k + 2]

    for d in range(1, 8):
        along_z(d).wait_send()
        share(d).wait_send()
    for n in range(4):
        along_x(n).wait_send()
        across(n).wait_send()
    for n in range(2):
        relay(n).wait_send()
    for d in range(1, 4):
        group(d, 0, 0).wait_send()

    def sent(h, e):
        return link(chunks.at[h, e], chunks.at[h, e], ry_send.at[h, e], ry_recv.at[0], other)

    @pl.when(primary)
    def _():
        sent(mine, 1 - c).wait_send()
        for e in range(2):
            sent(1 - mine, e).wait_send()

    @pl.when(secondary)
    def _():
        group(0, 0, 0).wait_send()
        for h in range(2):
            for e in range(2):
                sent(h, e).wait_send()


def per_device(targets, sources, kpt_coord):
    tables = [jnp.asarray(a) for a in host_tables()]
    vmem = pl.BlockSpec(memory_space=pltpu.VMEM)
    anywhere = pl.BlockSpec(memory_space=pl.ANY)
    sems = pltpu.SemaphoreType.DMA
    out = pl.pallas_call(
        exchange,
        in_specs=[anywhere] * 10,
        out_specs=vmem,
        out_shape=jax.ShapeDtypeStruct((2, 3456), F32),
        scratch_shapes=[
            pltpu.SMEM((3, 8), jnp.int32),
            pltpu.VMEM((2, 3456), BF16),
            pltpu.VMEM((1728, 128), BF16),
        ]
        + [pltpu.VMEM(a.shape, BF16) for a in tables]
        + [
            pltpu.VMEM((64, 128), F32),
            pltpu.VMEM((64, 128), BF16),
            pltpu.VMEM((8, 64, 128), BF16),
            pltpu.VMEM((2, 2, 8, 64, 128), BF16),
            pltpu.VMEM((1744, 128), F32),
            pltpu.VMEM((ROWS, NG * NG), BF16),
            pltpu.VMEM((NG, ROWS, 128), BF16),
            pltpu.VMEM((4, 2, ROWS, NG * NG), BF16),
            pltpu.VMEM((BATCH, NG, ROWS, 128), BF16),
            pltpu.VMEM((BATCH * SPAN, 128), F32),
            pltpu.VMEM((BATCH * SPAN, 128), F32),
            pltpu.VMEM((BATCH, NG, 128), F32),
            pltpu.VMEM((BATCH, NG, 128), F32),
            pltpu.VMEM((NG, ROWS, 128), F32),
            pltpu.VMEM((2, 2, 8, 64, 128), BF16),
            pltpu.VMEM((8, 4, 64, 128), BF16),
            pltpu.VMEM((8, 64, 128), BF16),
            pltpu.VMEM((8, 64, 128), BF16),
            sems((10,)), sems((8,)), sems((8,)), sems((4,)), sems((4, 2)), sems((6,)), sems((6,)),
            sems((4,)), sems((4,)), sems((2, 2)), sems((8,)), sems((8,)), sems((8,)),
        ],
        compiler_params=pltpu.CompilerParams(
            collective_id=0, has_side_effects=True, vmem_limit_bytes=62 * 2**20
        ),
    )(
        kpt_coord.T,
        targets.reshape(2, 3456),
        sources.reshape(2, 864, 128).transpose(1, 0, 2).reshape(1728, 128),
        *tables,
    )
    return out.reshape(1, 1, 2, 3456)


def solution(mesh):
    in_specs = (P("kpt", None, None, "band"), P("kpt", "band", None, None), P())
    out_specs = P("kpt", None, None, "band")
    return jax.shard_map(per_device, mesh=mesh, in_specs=in_specs, out_specs=out_specs, check_vma=False)
```

time: 842 us -> 55.9 us (0.07); the launches traced: 832 us -> 55.8 us
  waiting for transfers between devices: 332 us -> 0 us
  local copies, waits for them, and re-layouts: 286 us -> 1.36 us
  other arithmetic: 108 us -> 0 us
  Pallas kernels: 0 us -> 54.4 us
  blocking collectives: 47 us -> 0 us
  matrix products: 40.6 us -> 0 us
  between operations: 14.9 us -> 0.01 us
    unnamed x2 -> x0, waiting for transfers between devices: 285 us -> none
    unnamed x104 -> x1, local copies, waits for them, and re-layouts: 118 us -> 1.36 us
    another operation x56 -> x0, local copies, waits for them, and re-layouts: 83.1 us -> none
    another operation x13 -> x0, other arithmetic: 67.5 us -> none
    pallas_call x0 -> x1, Pallas kernels: none -> 54.4 us  [per_device(): pl.pallas_call(exchange, in_specs=[anywhere] * 10, out_specs=vmem, out_sh...]
    ppermute x7 -> x0, waiting for transfers between devices: 47.2 us -> none  [passed_along(): return lax.ppermute(block, axis, route)]
    all_gather x1 -> x0, blocking collectives: 47 us -> none  [per_device(): whole_targets = lax.all_gather(targets[0], 'band', axis=2, tiled=True)]
    dot_general x48 -> x0, matrix products: 40.6 us -> none  [transform(): jnp.einsum('pqmn,tqnc->tpcm', matrix, current, preferred_element_type=jnp...]
  transfers between devices with their start and end apart: 8 -> 0, of which waited for: 6 -> 0; matrix products, arithmetic and copies ran while one was open for 8% -> 0% of each run, Pallas kernels for 0% -> 0%
where the time goes in v3:
time: 55.9 us; the launch traced here: 55.8 us
  Pallas kernels  54.4 us (97%)
  local copies, waits for them, and re-layouts  1.36 us (2%)
    pallas_call x1, Pallas kernels, per_device(): pl.pallas_call(exchange, in_specs=[anywhere] * 10, out_specs=vmem, out_sh...  54.4 us
    unnamed x1, local copies, waits for them, and re-layouts  1.36 us

profile of v3, /device:TPU:1, one launch (start us, length us, event | category | flops | bytes accessed | tf_op | source)
XLA Modules:
  0.0 55.8 jit_solution(10092506473956092884)
XLA Ops:
  0.0 54.4 %shard_map.100 = f32[2,3456]{1,0:T(2,128)} custom-call(s32[3,8]{1,0:T(4,128)} %bitcast.11, bf16[2,3456]{1,0:T(2,128)(2,1)} %bitcast.10, bf16[1728,128]{1,0:T(8,128)(2,1)} %bitcast.8, bf16[96,96]{1,0:T(8,128)(2,1)} %constant.14.clone.fwd_hbm, bf16[96,96]{1,0:T(8,128)(2,1)} %constant.15.clone.bwd_hbm, bf16[256,256]{1,0:T(8,128)(2,1)} %constant.16.clone.zfwd_hbm, ...), custom_call_target="tpu_custom_call" | custom-call | tf_op jit(solution)/shard_map/pallas_call | solution.py:471
  54.4 1.4 %copy.13 = f32[1,1,2,3456]{3,2,1,0:T(2,128)} copy(f32[1,1,2,3456]{3,2,1,0:T(2,128)} %bitcast.9) | data formatting | bytes 55296

commit v4 on v3

--- a/solution.py
+++ b/solution.py
@@ -176,12 +176,13 @@
         part, place, to = legs[n]
         return link(sources.at[place, c, part], sources.at[3, c, part], s_send.at[4 + n], s_recv.at[4 + n], to)
 
-    def across(num):
-        return link(sources.at[num, c], sources.at[num, c], c_send.at[num], c_recv.at[num], other)
+    def across(n):
+        held = sources.at[0, c] if n == 6 else sources.at[(1, 2, 1, 2, 3, 3)[n], c, (low, high)[(0, 1, 1, 0, 0, 1)[n]]]
+        return link(held, held, c_send.at[n], c_recv.at[n], other)
 
     for n in range(4):
         along_x(n).start()
-    across(0).start()
+    across(6).start()
     total[...] = jnp.zeros_like(total)
 
     for d in (1, 7, 2, 6, 3, 5, 4):
@@ -189,10 +190,9 @@
         from_z = (z + 8 - d) % 8
         spread_y(carried.at[from_z], from_z)
 
-    along_x(0).wait_recv()
-    relay(0).start()
-    along_x(1).wait_recv()
-    relay(1).start()
+    for n in range(2):
+        along_x(n).wait_recv()
+        across(n).start()
 
     def group(d, h, e):
         whole = slots.at[h, e]
@@ -228,6 +228,11 @@
 
     for copy in fetched[2:]:
         copy.wait()
+    for n in range(2, 4):
+        along_x(n).wait_recv()
+        across(n).start()
+    for n in range(2):
+        relay(n).start()
 
     def spread_out(read, table, copies, store):
         for g in range(6):
@@ -245,9 +250,6 @@
 
     spread_out(lambda i, lanes: dense[:, lanes], one_ref, 1, set_target)
 
-    along_x(2).wait_recv()
-    across(1).start()
-
     lane = lax.broadcasted_iota(jnp.int32, (NG, 128), 1)
     row = lax.broadcasted_iota(jnp.int32, (NG, 128), 0)
 
@@ -261,15 +263,13 @@
     zbackward = zbwd_ref[...]
 
     def prepare(num, carry):
-        @pl.when(num == 2)
-        def _():
-            along_x(3).wait_recv()
-            across(2).start()
-            relay(0).wait_recv()
-            relay(1).wait_recv()
-            across(3).start()
-
-        across(num).wait_recv()
+        for place, needed in enumerate(((6,), (0, 2), (1, 3), (4, 5))):
+
+            @pl.when(num == place)
+            def _():
+                for n in needed:
+                    across(n).wait_recv()
+
         at = num % BATCH
 
         def set_source(cell, block):
@@ -371,6 +371,15 @@
                 return carry
 
             lax.fori_loop(0, BATCH * count, one, 0)
+
+            if phase is through_spectrum:
+
+                @pl.when(num == 0)
+                def _():
+                    for n in range(2):
+                        relay(n).wait_recv()
+                        across(4 + n).start()
+
         return carry
 
     lax.fori_loop(0, 4 // BATCH, batch, 0)
@@ -440,6 +449,7 @@
         share(d).wait_send()
     for n in range(4):
         along_x(n).wait_send()
+    for n in range(7):
         across(n).wait_send()
     for n in range(2):
         relay(n).wait_send()
@@ -499,7 +509,7 @@
             pltpu.VMEM((8, 64, 128), BF16),
             pltpu.VMEM((8, 64, 128), BF16),
             sems((10,)), sems((8,)), sems((8,)), sems((4,)), sems((4, 2)), sems((6,)), sems((6,)),
-            sems((4,)), sems((4,)), sems((2, 2)), sems((8,)), sems((8,)), sems((8,)),
+            sems((7,)), sems((7,)), sems((2, 2)), sems((8,)), sems((8,)), sems((8,)),
         ],
         compiler_params=pltpu.CompilerParams(
             collective_id=0, has_side_effects=True, vmem_limit_bytes=62 * 2**20

time: 55.9 us -> 53.6 us (0.959)
  Pallas kernels: 54.4 us -> 52.1 us
    pallas_call x1, Pallas kernels: 54.4 us -> 52.1 us  [per_device(): pl.pallas_call(exchange, in_specs=[anywhere] * 10, out_specs=vmem, out_sh...]
where the time goes in v4:
time: 53.6 us; the launch traced here: 53.5 us
  Pallas kernels  52.1 us (97%)
  local copies, waits for them, and re-layouts  1.36 us (3%)
    pallas_call x1, Pallas kernels, per_device(): pl.pallas_call(exchange, in_specs=[anywhere] * 10, out_specs=vmem, out_sh...  52.1 us
    unnamed x1, local copies, waits for them, and re-layouts  1.36 us

profile of v4, /device:TPU:1, one launch (start us, length us, event | category | flops | bytes accessed | tf_op | source)
XLA Modules:
  0.0 53.5 jit_solution(16870283649909785804)
XLA Ops:
  0.0 52.1 %shard_map.100 = f32[2,3456]{1,0:T(2,128)} custom-call(s32[3,8]{1,0:T(4,128)} %bitcast.11, bf16[2,3456]{1,0:T(2,128)(2,1)} %bitcast.10, bf16[1728,128]{1,0:T(8,128)(2,1)} %bitcast.8, bf16[96,96]{1,0:T(8,128)(2,1)} %constant.14.clone.fwd_hbm, bf16[96,96]{1,0:T(8,128)(2,1)} %constant.15.clone.bwd_hbm, bf16[256,256]{1,0:T(8,128)(2,1)} %constant.16.clone.zfwd_hbm, ...), custom_call_target="tpu_custom_call" | custom-call | tf_op jit(solution)/shard_map/pallas_call | solution.py:481
  52.1 1.4 %copy.13 = f32[1,1,2,3456]{3,2,1,0:T(2,128)} copy(f32[1,1,2,3456]{3,2,1,0:T(2,128)} %bitcast.9) | data formatting | bytes 55296

commit v5 on v4

--- a/solution.py
+++ b/solution.py
@@ -16,7 +16,7 @@
 GROUP1 = 24
 GROUP2 = 24
 GROUP3 = 24
-BATCH = 2
+BATCH = 4
 SPAN = NG * PITCH
 SPREAD_FROM = (0, 0, 128, 256)
 SPREAD_WIDE = (128, 256, 256, 128)
@@ -128,6 +128,20 @@
         staged[2 * k:2 * k + 2, :] = slice_ref[:, 128 * k:128 * k + 128].astype(F32)
     piece[...] = staged[...].astype(BF16)
 
+    fetched[1].wait()
+
+    def densify(raw, store):
+        for p in range(2):
+            for col in range(18):
+                store(p, col, raw[pl.ds(2 * col + p, NG, stride=36), :].astype(BF16))
+
+    rows_f32[pl.ds(0, 2 * 864), :] = raw_ref[...].astype(F32)
+
+    def keep_source(p, col, block):
+        sources[0, c, p * NG:(p + 1) * NG, col * 128:(col + 1) * 128] = block
+
+    densify(rows_f32, keep_source)
+
     pl.semaphore_wait(barrier, len(peers))
 
     def along_z(d):
@@ -148,22 +162,6 @@
 
     for d in (4, 3, 5, 2, 6, 1, 7):
         along_z(d).start()
-    spread_y(piece, z)
-
-    fetched[1].wait()
-
-    def densify(raw, store):
-        for p in range(2):
-            for col in range(18):
-                store(p, col, raw[pl.ds(2 * col + p, NG, stride=36), :].astype(BF16))
-
-    rows_f32[pl.ds(0, 2 * 864), :] = raw_ref[...].astype(F32)
-
-    def keep_source(p, col, block):
-        sources[0, c, p * NG:(p + 1) * NG, col * 128:(col + 1) * 128] = block
-
-    densify(rows_f32, keep_source)
-
     low = pl.ds(0, NG)
     high = pl.ds(NG, NG)
     legs = ((low, 1, x_up), (high, 2, x_down), (high, 1, x_up), (low, 2, x_down))
@@ -182,6 +180,7 @@
 
     for n in range(4):
         along_x(n).start()
+    spread_y(piece, z)
     across(6).start()
     total[...] = jnp.zeros_like(total)
 
@@ -194,45 +193,8 @@
         along_x(n).wait_recv()
         across(n).start()
 
-    def group(d, h, e):
-        whole = slots.at[h, e]
-        return link(whole, whole, gy_send.at[d], gy_recv.at[d, e], other)
-
-    @pl.when(primary)
-    def _():
-        carried[z] = piece[...]
-        slots[mine, c] = carried[...]
-        group(0, mine, 1 - c).wait_recv()
-        for e in range(2):
-            group(2, 1 - mine, e).wait_recv()
-
-    @pl.when(secondary)
-    def _():
-        for e in range(2):
-            group(1, ((y + 3) % 4) // 2, e).wait_recv()
-            group(3, ((y + 1) % 4) // 2, e).wait_recv()
-
-    def unpack(z_, carry):
-        for h in range(2):
-            for e in range(2):
-                start = 54 * (4 * z_ + 2 * h + e)
-                rows_f32[pl.ds(start, 54), :] = slots[h, e, z_].astype(F32)[:54]
-        return carry
-
-    lax.fori_loop(0, 8, unpack, 0)
-
-    def keep_target(p, col, block):
-        dense[p * NG:(p + 1) * NG, col * 128:(col + 1) * 128] = block
-
-    densify(rows_f32, keep_target)
-
     for copy in fetched[2:]:
         copy.wait()
-    for n in range(2, 4):
-        along_x(n).wait_recv()
-        across(n).start()
-    for n in range(2):
-        relay(n).start()
 
     def spread_out(read, table, copies, store):
         for g in range(6):
@@ -245,11 +207,6 @@
                 store(8 * g + 2 * k, wide[:, :128])
                 store(8 * g + 2 * k + 1, wide[:, 128:])
 
-    def set_target(cell, block):
-        targ[cell] = block
-
-    spread_out(lambda i, lanes: dense[:, lanes], one_ref, 1, set_target)
-
     lane = lax.broadcasted_iota(jnp.int32, (NG, 128), 1)
     row = lax.broadcasted_iota(jnp.int32, (NG, 128), 0)
 
@@ -257,20 +214,16 @@
         return jnp.where(i < NG // 2, i, i - NG).astype(F32)
 
     scale = 4.0 * math.pi / float(NG**3)
-    forward = fwd_ref[...]
-    backward = bwd_ref[...]
-    zforward = zfwd_ref[...]
-    zbackward = zbwd_ref[...]
-
-    def prepare(num, carry):
+
+    def prepare(num):
         for place, needed in enumerate(((6,), (0, 2), (1, 3), (4, 5))):
 
-            @pl.when(num == place)
+            @pl.when(jnp.equal(num, place))
             def _():
                 for n in needed:
                     across(n).wait_recv()
 
-        at = num % BATCH
+        at = num
 
         def set_source(cell, block):
             src[at, cell] = block
@@ -287,7 +240,55 @@
         fz = frequency(lane % 64) + offset(2)
         coul[at] = 0.04 * (fx * fx)
         base[at] = 0.04 * (fy * fy + fz * fz) + 0.25
+
+    prepare(0)
+    forward = fwd_ref[...]
+    backward = bwd_ref[...]
+    zforward = zfwd_ref[...]
+    zbackward = zbwd_ref[...]
+
+    def group(d, h, e):
+        whole = slots.at[h, e]
+        return link(whole, whole, gy_send.at[d], gy_recv.at[d, e], other)
+
+    @pl.when(primary)
+    def _():
+        carried[z] = piece[...]
+        slots[mine, c] = carried[...]
+        group(0, mine, 1 - c).wait_recv()
+        for e in range(2):
+            group(2, 1 - mine, e).wait_recv()
+
+    @pl.when(secondary)
+    def _():
+        for e in range(2):
+            group(1, ((y + 3) % 4) // 2, e).wait_recv()
+            group(3, ((y + 1) % 4) // 2, e).wait_recv()
+
+    def unpack(z_, carry):
+        for h in range(2):
+            for e in range(2):
+                start = 54 * (4 * z_ + 2 * h + e)
+                rows_f32[pl.ds(start, 54), :] = slots[h, e, z_].astype(F32)[:54]
         return carry
+
+    lax.fori_loop(0, 8, unpack, 0)
+
+    def keep_target(p, col, block):
+        dense[p * NG:(p + 1) * NG, col * 128:(col + 1) * 128] = block
+
+    densify(rows_f32, keep_target)
+
+    for n in range(2, 4):
+        along_x(n).wait_recv()
+        across(n).start()
+    for n in range(2):
+        relay(n).start()
+
+    def set_target(cell, block):
+        targ[cell] = block
+
+    spread_out(lambda i, lanes: dense[:, lanes], one_ref, 1, set_target)
 
     def into_spectrum(at, i):
         mixed = []
@@ -361,28 +362,39 @@
                 total[cell, :NG, :] += sr * pr - si * pi
                 total[cell, NG:, :] += sr * pi + si * pr
 
-    def batch(num, carry):
-        lax.fori_loop(num * BATCH, num * BATCH + BATCH, prepare, 0)
-        for phase, size in ((into_spectrum, GROUP1), (through_spectrum, GROUP2), (out_of_spectrum, GROUP3)):
-            count = NG // 2 // size
-
-            def one(k, carry):
-                phase(k // count, k % count)
-                return carry
-
-            lax.fori_loop(0, BATCH * count, one, 0)
-
-            if phase is through_spectrum:
-
-                @pl.when(num == 0)
-                def _():
-                    for n in range(2):
-                        relay(n).wait_recv()
-                        across(4 + n).start()
-
+    def begin(num, carry):
+        @pl.when(num > 0)
+        def _():
+            prepare(num)
+
+        for i in range(NG // 2 // GROUP1):
+            into_spectrum(num, i)
         return carry
 
-    lax.fori_loop(0, 4 // BATCH, batch, 0)
+    def middle(num, carry):
+        @pl.when(num == 2)
+        def _():
+            for n in range(2):
+                relay(n).wait_recv()
+                across(4 + n).start()
+
+        for i in range(NG // 2 // GROUP2):
+            through_spectrum(num, i)
+        return carry
+
+    def finish(num, carry):
+        for i in range(NG // 2 // GROUP3):
+            out_of_spectrum(num, i)
+        return carry
+
+    def stage(num, carry):
+        start, stop = 3 * num, 3 + num
+        lax.fori_loop(start, stop, begin, 0)
+        lax.fori_loop(start, stop, middle, 0)
+        return carry
+
+    lax.fori_loop(0, 2, stage, 0)
+    lax.fori_loop(0, 4, finish, 0)
 
     for g in range(6):
         for chunk in range(3):

time: 53.6 us -> 52.1 us (0.972)
  Pallas kernels: 52.1 us -> 50.6 us
    pallas_call x1, Pallas kernels: 52.1 us -> 50.6 us  [per_device(): pl.pallas_call(exchange, in_specs=[anywhere] * 10, out_specs=vmem, out_sh...]
where the time goes in v5:
time: 52.1 us; the launch traced here: 51.9 us
  Pallas kernels  50.6 us (97%)
  local copies, waits for them, and re-layouts  1.36 us (3%)
    pallas_call x1, Pallas kernels, per_device(): pl.pallas_call(exchange, in_specs=[anywhere] * 10, out_specs=vmem, out_sh...  50.6 us
    unnamed x1, local copies, waits for them, and re-layouts  1.36 us

profile of v5, /device:TPU:1, one launch (start us, length us, event | category | flops | bytes accessed | tf_op | source)
XLA Modules:
  0.0 51.9 jit_solution(7107223838131807876)
XLA Ops:
  0.0 50.6 %shard_map.100 = f32[2,3456]{1,0:T(2,128)} custom-call(s32[3,8]{1,0:T(4,128)} %bitcast.11, bf16[2,3456]{1,0:T(2,128)(2,1)} %bitcast.10, bf16[1728,128]{1,0:T(8,128)(2,1)} %bitcast.8, bf16[96,96]{1,0:T(8,128)(2,1)} %constant.14.clone.fwd_hbm, bf16[96,96]{1,0:T(8,128)(2,1)} %constant.15.clone.bwd_hbm, bf16[256,256]{1,0:T(8,128)(2,1)} %constant.16.clone.zfwd_hbm, ...), custom_call_target="tpu_custom_call" | custom-call | tf_op jit(solution)/shard_map/pallas_call | solution.py:493
  50.6 1.4 %copy.13 = f32[1,1,2,3456]{3,2,1,0:T(2,128)} copy(f32[1,1,2,3456]{3,2,1,0:T(2,128)} %bitcast.9) | data formatting | bytes 55296

commit v6 on v5

--- a/solution.py
+++ b/solution.py
@@ -160,8 +160,17 @@
         def _():
             along_y(0, held, z_).start()
 
-    for d in (4, 3, 5, 2, 6, 1, 7):
-        along_z(d).start()
+    def outer_first(i):
+        return jnp.where(i % 2 == 0, 4 + i // 2, 4 - (i + 1) // 2)
+
+    def repeat(start, stop, act):
+        def one(i, carry):
+            act(i)
+            return carry
+
+        lax.fori_loop(start, stop, one, 0)
+
+    repeat(0, 7, lambda i: along_z(outer_first(i)).start())
     low = pl.ds(0, NG)
     high = pl.ds(NG, NG)
     legs = ((low, 1, x_up), (high, 2, x_down), (high, 1, x_up), (low, 2, x_down))
@@ -184,10 +193,13 @@
     across(6).start()
     total[...] = jnp.zeros_like(total)
 
-    for d in (1, 7, 2, 6, 3, 5, 4):
+    def forward_slice(i):
+        d = jnp.where(i % 2 == 0, 1 + i // 2, 7 - i // 2)
         along_z(d).wait_recv()
         from_z = (z + 8 - d) % 8
         spread_y(carried.at[from_z], from_z)
+
+    repeat(0, 7, forward_slice)
 
     for n in range(2):
         along_x(n).wait_recv()
@@ -251,6 +263,12 @@
         whole = slots.at[h, e]
         return link(whole, whole, gy_send.at[d], gy_recv.at[d, e], other)
 
+    for n in range(2, 4):
+        along_x(n).wait_recv()
+        across(n).start()
+    for n in range(2):
+        relay(n).start()
+
     @pl.when(primary)
     def _():
         carried[z] = piece[...]
@@ -279,11 +297,6 @@
 
     densify(rows_f32, keep_target)
 
-    for n in range(2, 4):
-        along_x(n).wait_recv()
-        across(n).start()
-    for n in range(2):
-        relay(n).start()
 
     def set_target(cell, block):
         targ[cell] = block
@@ -407,9 +420,8 @@
         where = device(x, (y + k) % 4, z, e)
         return link(chunks.at[h, e, z_], arrived.at[z_, k], ry_send.at[h, e], ry_recv.at[z_], where)
 
-    order = (4, 3, 5, 2, 6, 1, 7, 0)
-    for d in order:
-        z_ = (z + d) % 8
+    def send_slots(i):
+        z_ = (z + outer_first(i)) % 8
         for h in range(2):
             for e in range(2):
                 start = 54 * (4 * z_ + 2 * h + e)
@@ -428,13 +440,13 @@
                 to_owner(((y + 1) % 4) // 2, e, z_, 1).start()
                 to_owner(((y + 3) % 4) // 2, e, z_, 3).start()
 
+    repeat(0, 8, send_slots)
+
     def share(d):
         to_z = (z + d) % 8
         return link(parts.at[to_z], finals.at[d], rz_send.at[d], rz_recv.at[d], device(x, y, to_z, c))
 
-    for d in order:
-        z_ = (z + d) % 8
-
+    def collect(z_):
         @pl.when(primary)
         def _():
             three = arrived.at[z_, pl.ds(1, 3)]
@@ -444,21 +456,27 @@
         def _():
             link(arrived.at[z_], arrived.at[z_], ry_send.at[0, 0], ry_recv.at[z_], other).wait_recv()
 
-        summed = sum([arrived[z_, k].astype(F32) for k in range(1, 4)], arrived[z_, 0].astype(F32))
-        if d:
-            parts[z_] = summed.astype(BF16)
-            share(d).start()
-
-    for d in range(1, 8):
-        share(d).wait_recv()
-        summed = summed + finals[d].astype(F32)
-    result = summed * (-1.0 / 8.0)
+        return sum([arrived[z_, k].astype(F32) for k in range(1, 4)], arrived[z_, 0].astype(F32))
+
+    def pass_on(i):
+        d = outer_first(i)
+        z_ = (z + d) % 8
+        parts[z_] = collect(z_).astype(BF16)
+        share(d).start()
+
+    repeat(0, 7, pass_on)
+    summed = collect(z)
+    repeat(1, 8, lambda d: share(d).wait_recv())
+    summed = sum([finals[d].astype(F32) for d in range(1, 8)], summed)
+    result = summed
     for k in range(27):
         out_ref[:, 128 * k:128 * k + 128] = result[2 * k:2 * k + 2]
 
-    for d in range(1, 8):
+    def settle(d):
         along_z(d).wait_send()
         share(d).wait_send()
+
+    repeat(1, 8, settle)
     for n in range(4):
         along_x(n).wait_send()
     for n in range(7):
@@ -532,7 +550,7 @@
         sources.reshape(2, 864, 128).transpose(1, 0, 2).reshape(1728, 128),
         *tables,
     )
-    return out.reshape(1, 1, 2, 3456)
+    return (out * (-1.0 / 8.0)).reshape(1, 1, 2, 3456)
 
 
 def solution(mesh):

time: 52.1 us -> 52.1 us (level)
  other arithmetic: 0 us -> 1.37 us
  local copies, waits for them, and re-layouts: 1.36 us -> 0 us
    reshape x0 -> x1, other arithmetic: none -> 1.37 us  [per_device(): return (out * (-1.0 / 8.0)).reshape(1, 1, 2, 3456)]
    unnamed x1 -> x0, local copies, waits for them, and re-layouts: 1.36 us -> none
where the time goes in v6:
time: 52.1 us; the launch traced here: 51.9 us
  Pallas kernels  50.5 us (97%)
  other arithmetic  1.37 us (3%)
    pallas_call x1, Pallas kernels, per_device(): pl.pallas_call(exchange, in_specs=[anywhere] * 10, out_specs=vmem, out_sh...  50.5 us
    reshape x1, other arithmetic, per_device(): return (out * (-1.0 / 8.0)).reshape(1, 1, 2, 3456)  1.37 us

profile of v6, /device:TPU:1, one launch (start us, length us, event | category | flops | bytes accessed | tf_op | source)
XLA Modules:
  0.0 51.9 jit_solution(9633681333241211636)
XLA Ops:
  0.0 50.5 %shard_map.100 = f32[2,3456]{1,0:T(2,128)} custom-call(s32[3,8]{1,0:T(4,128)} %bitcast.11, bf16[2,3456]{1,0:T(2,128)(2,1)} %bitcast.10, bf16[1728,128]{1,0:T(8,128)(2,1)} %bitcast.9, bf16[96,96]{1,0:T(8,128)(2,1)} %constant.16.clone.fwd_hbm, bf16[96,96]{1,0:T(8,128)(2,1)} %constant.17.clone.bwd_hbm, bf16[256,256]{1,0:T(8,128)(2,1)} %constant.18.clone.zfwd_hbm, ...), custom_call_target="tpu_custom_call" | custom-call | tf_op jit(solution)/shard_map/pallas_call | solution.py:511
  50.5 1.4 %multiply_bitcast_fusion = f32[1,1,2,3456]{3,2,1,0:T(2,128)} fusion(f32[2,3456]{1,0:T(2,128)} %shard_map.100), kind=kLoop, calls=%fused_computation | loop fusion | flops 6912 | bytes 55296 | tf_op jit(solution)/shard_map/reshape | solution.py:553

commit v7 on v6

--- a/solution.py
+++ b/solution.py
@@ -524,13 +524,13 @@
             pltpu.VMEM((64, 128), BF16),
             pltpu.VMEM((8, 64, 128), BF16),
             pltpu.VMEM((2, 2, 8, 64, 128), BF16),
-            pltpu.VMEM((1744, 128), F32),
+            pltpu.VMEM((1792, 128), F32),
             pltpu.VMEM((ROWS, NG * NG), BF16),
             pltpu.VMEM((NG, ROWS, 128), BF16),
             pltpu.VMEM((4, 2, ROWS, NG * NG), BF16),
             pltpu.VMEM((BATCH, NG, ROWS, 128), BF16),
-            pltpu.VMEM((BATCH * SPAN, 128), F32),
-            pltpu.VMEM((BATCH * SPAN, 128), F32),
+            pltpu.VMEM((BATCH * SPAN + 128, 128), F32),
+            pltpu.VMEM((BATCH * SPAN + 128, 128), F32),
             pltpu.VMEM((BATCH, NG, 128), F32),
             pltpu.VMEM((BATCH, NG, 128), F32),
             pltpu.VMEM((NG, ROWS, 128), F32),

time: 52.1 us -> 51.9 us (level)
  no operation moved by 1% of the time
where the time goes in v7:
time: 51.9 us; the launch traced here: 51.7 us
  Pallas kernels  50.4 us (97%)
  other arithmetic  1.37 us (3%)
    pallas_call x1, Pallas kernels, per_device(): pl.pallas_call(exchange, in_specs=[anywhere] * 10, out_specs=vmem, out_sh...  50.4 us
    reshape x1, other arithmetic, per_device(): return (out * (-1.0 / 8.0)).reshape(1, 1, 2, 3456)  1.37 us

profile of v7, /device:TPU:1, one launch (start us, length us, event | category | flops | bytes accessed | tf_op | source)
XLA Modules:
  0.0 51.7 jit_solution(6073146869060732654)
XLA Ops:
  0.0 50.4 %shard_map.100 = f32[2,3456]{1,0:T(2,128)} custom-call(s32[3,8]{1,0:T(4,128)} %bitcast.11, bf16[2,3456]{1,0:T(2,128)(2,1)} %bitcast.10, bf16[1728,128]{1,0:T(8,128)(2,1)} %bitcast.9, bf16[96,96]{1,0:T(8,128)(2,1)} %constant.16.clone.fwd_hbm, bf16[96,96]{1,0:T(8,128)(2,1)} %constant.17.clone.bwd_hbm, bf16[256,256]{1,0:T(8,128)(2,1)} %constant.18.clone.zfwd_hbm, ...), custom_call_target="tpu_custom_call" | custom-call | tf_op jit(solution)/shard_map/pallas_call | solution.py:511
  50.4 1.4 %multiply_bitcast_fusion = f32[1,1,2,3456]{3,2,1,0:T(2,128)} fusion(f32[2,3456]{1,0:T(2,128)} %shard_map.100), kind=kLoop, calls=%fused_computation | loop fusion | flops 6912 | bytes 55296 | tf_op jit(solution)/shard_map/reshape | solution.py:553

commit v8 on v7

--- a/solution.py
+++ b/solution.py
@@ -170,7 +170,6 @@
 
         lax.fori_loop(start, stop, one, 0)
 
-    repeat(0, 7, lambda i: along_z(outer_first(i)).start())
     low = pl.ds(0, NG)
     high = pl.ds(NG, NG)
     legs = ((low, 1, x_up), (high, 2, x_down), (high, 1, x_up), (low, 2, x_down))
@@ -189,6 +188,7 @@
 
     for n in range(4):
         along_x(n).start()
+    repeat(0, 7, lambda i: along_z(outer_first(i)).start())
     spread_y(piece, z)
     across(6).start()
     total[...] = jnp.zeros_like(total)

time: 51.9 us -> 51.9 us (level)
  no operation moved by 1% of the time
where the time goes in v8:
time: 51.9 us; the launch traced here: 51.7 us
  Pallas kernels  50.4 us (97%)
  other arithmetic  1.37 us (3%)
    pallas_call x1, Pallas kernels, per_device(): pl.pallas_call(exchange, in_specs=[anywhere] * 10, out_specs=vmem, out_sh...  50.4 us
    reshape x1, other arithmetic, per_device(): return (out * (-1.0 / 8.0)).reshape(1, 1, 2, 3456)  1.37 us

profile of v8, /device:TPU:1, one launch (start us, length us, event | category | flops | bytes accessed | tf_op | source)
XLA Modules:
  0.0 51.7 jit_solution(14133087772043718187)
XLA Ops:
  0.0 50.4 %shard_map.100 = f32[2,3456]{1,0:T(2,128)} custom-call(s32[3,8]{1,0:T(4,128)} %bitcast.11, bf16[2,3456]{1,0:T(2,128)(2,1)} %bitcast.10, bf16[1728,128]{1,0:T(8,128)(2,1)} %bitcast.9, bf16[96,96]{1,0:T(8,128)(2,1)} %constant.16.clone.fwd_hbm, bf16[96,96]{1,0:T(8,128)(2,1)} %constant.17.clone.bwd_hbm, bf16[256,256]{1,0:T(8,128)(2,1)} %constant.18.clone.zfwd_hbm, ...), custom_call_target="tpu_custom_call" | custom-call | tf_op jit(solution)/shard_map/pallas_call | solution.py:511
  50.4 1.4 %multiply_bitcast_fusion = f32[1,1,2,3456]{3,2,1,0:T(2,128)} fusion(f32[2,3456]{1,0:T(2,128)} %shard_map.100), kind=kLoop, calls=%fused_computation | loop fusion | flops 6912 | bytes 55296 | tf_op jit(solution)/shard_map/reshape | solution.py:553
